TPU v7x, 512 devices: a whole 4x8x8 slice. The times are simulated.
512 devices in a mesh: seq: 8 (over z), dec: 32 (over y, x), rep: 2 (over core).
Axes of the slice: x: 4, y: 8, z: 8, core: 2. Of those that a mesh axis runs over, the one named last changes fastest.
Arguments:
- queries: bfloat16 [64, 128, 8192], P(('rep', 'dec'), 'seq'), parts along dimension 0, may hold values from -360 to 360
- slab_kv: bfloat16 [64, 128, 2048], P(('rep', 'dec'), 'seq'), parts along dimension 0, may hold values from -6 to 6
- prefix_kv: bfloat16 [2048, 2048], P(('rep', 'dec'), 'seq'), parts along dimension 0, may hold values from -6 to 6
- owners: int32 [16, 32], P(('rep', 'seq')), parts along dimension 0, may hold values from 0 to 31, as said below
- offset: int32 [2], P('rep'), parts along dimension 0, may hold values from 512 to 1024
Outputs:
- attention: bfloat16 [64, 128, 8192], P(('rep', 'dec'), 'seq'), parts along dimension 0
- page_store: bfloat16 [16, 32, 2, 128, 256], P(('rep', 'seq'), 'dec'), parts along dimension 0
- page_scales: bfloat16 [16, 32, 2, 2], P(('rep', 'seq'), 'dec'), parts along dimension 0
There are 2 independent parts, one for each index of `rep`. A program takes and returns all parts, laid end to end along the dimension named above; each array names one. Nothing has to cross between parts.
Inputs may be any that keep to these rules, and one draw needn't show every extreme that they name: `owners`: for each head no owner holds more than 2 pages, and some owner holds exactly 2 pages of every head.
All inputs are finite; a program needn't handle non-finite values. Where the computation divides by a largest or mean magnitude, that divisor is 1e-20 or more.
Results may differ from a plain program's by a relative error of at most 0.025.
The roundings to bfloat16 on the way count: a program that leaves them out, or rounds other values in their place, can miss the bound.
Values may be sent and summed in bfloat16 or wider, within the bound.
No kernel may reach another device: no remote copies, remote signals or barrier semaphores. Data moves between devices by JAX's collectives and lax.ppermute only.
A program may use at most 64 MiB of HBM per device.

v0:
```python
import math

import jax
import jax.numpy as jnp
from jax import lax
from jax.sharding import PartitionSpec as P

HQ = 64
KVH = 8
HD = 128
PAGE = 128


rope_base = 1000000.0
tiny = 1e-06
masked = -1e30


def rotate(values, position):
    width = values.shape[-1]
    middle = width // 2
    inverse = rope_base ** (-(jnp.arange(middle, dtype=jnp.float32) * 2.0 / width))
    angles = position.astype(jnp.float32)[:, None] * inverse[None, :]
    cosine = jnp.cos(angles)[:, None, :]
    sinus = jnp.sin(angles)[:, None, :]
    leading = values[..., :middle].astype(jnp.float32)
    trailing = values[..., middle:].astype(jnp.float32)
    return jnp.concatenate(
        [leading * cosine - trailing * sinus, trailing * cosine + leading * sinus], axis=-1
    )


def quantize(rows_kv, heads, width, page_len):
    number = rows_kv.shape[0] // page_len
    grouped = rows_kv.reshape(number, page_len, heads, 2, width).astype(jnp.float32)
    largest = jnp.max(jnp.abs(grouped), axis=(1, 4))
    scaled = (grouped / (largest[:, None, :, :, None] + tiny)).astype(jnp.bfloat16)
    scaled = scaled.transpose(2, 0, 1, 3, 4).reshape(heads, number, page_len * 2 * width)
    return (scaled, largest.transpose(1, 0, 2).astype(jnp.bfloat16))


def page_ranks(targets):
    number = targets.shape[1]
    matching = targets[:, :, None] == targets[:, None, :]
    indices = jnp.arange(number, dtype=jnp.int32)
    earlier = indices[:, None] > indices[None, :]
    return jnp.sum((matching & earlier[None]).astype(jnp.int32), axis=2)


def place_pages(carry, pieces, targets, ranks_local, myself):
    page_values, page_tops = pieces
    capacity = carry[1].shape[1]
    chosen = (targets == myself)[:, None, :] & (
        ranks_local[:, None, :] == jnp.arange(capacity, dtype=jnp.int32)[None, :, None]
    )
    chosen = chosen.astype(jnp.bfloat16)
    stored = jnp.einsum("gsj,gjc->gsc", chosen, page_values, preferred_element_type=jnp.float32)
    scales = jnp.einsum("gsj,gjc->gsc", chosen, page_tops, preferred_element_type=jnp.float32)
    return (stored, scales)


def on_device(queries, slab_kv, prefix_kv, owners, offset):
    asked, kv_rows = (
        lax.all_to_all(queries, "seq", split_axis=2, concat_axis=1, tiled=True),
        lax.all_to_all(slab_kv, "seq", split_axis=2, concat_axis=1, tiled=True),
    )
    rows = asked.shape[1]
    width = HD
    heads_local = kv_rows.shape[2] // (2 * width)
    group = HQ // KVH
    myself = lax.axis_index("dec")
    owner_count = lax.axis_size("dec")
    begin = offset[0]
    slab_index = myself * rows + jnp.arange(rows, dtype=jnp.int32)
    position = begin + slab_index
    turned = rotate(asked.reshape(rows, heads_local * group, width), position).astype(jnp.bfloat16)
    turned = (
        turned.reshape(rows, heads_local, group, width)
        .transpose(1, 2, 0, 3)
        .reshape(heads_local, group * rows, width)
    )
    row_index = jnp.tile(slab_index, group)
    paired = kv_rows.reshape(rows, heads_local, 2, width)
    fresh_keys = rotate(paired[:, :, 0], position).astype(jnp.bfloat16)
    own_rows = jnp.stack([fresh_keys, paired[:, :, 1]], axis=2).reshape(
        rows, heads_local * 2 * width
    )
    scale = width ** (-0.5)
    prefix_whole = lax.all_gather(prefix_kv, "dec", axis=0, tiled=True)
    slab_whole = lax.all_gather(own_rows, "dec", axis=0, tiled=True)
    prefix_len = prefix_whole.shape[0]
    key_rows = jnp.concatenate([prefix_whole, slab_whole], axis=0)
    key_total = key_rows.shape[0]
    span = math.gcd(512, key_total)

    def visit_block(step, carry):
        running, mass, numer = carry
        first = (step * span).astype(jnp.int32)
        block_rows = lax.dynamic_slice_in_dim(key_rows, first, span, 0)
        split_rows = block_rows.reshape(span, heads_local, 2, width)
        key_index = first + jnp.arange(span, dtype=jnp.int32)
        allowed = jnp.where(
            (key_index < prefix_len)[None, :],
            (key_index < begin)[None, :],
            (key_index - prefix_len)[None, :] <= row_index[:, None],
        )
        scores = (
            jnp.einsum(
                "grd,ngd->grn", turned, split_rows[:, :, 0], preferred_element_type=jnp.float32
            )
            * scale
        )
        scores = jnp.where(allowed[None], scores, masked)
        highest = jnp.maximum(running, jnp.max(scores, axis=-1))
        weights = jnp.where(allowed[None], jnp.exp(scores - highest[..., None]), 0.0)
        factor = jnp.exp(running - highest)
        mass = mass * factor + jnp.sum(weights, axis=-1)
        numer = numer * factor[..., None] + jnp.einsum(
            "grn,ngd->grd",
            weights.astype(jnp.bfloat16),
            split_rows[:, :, 1],
            preferred_element_type=jnp.float32,
        )
        return (highest, mass, numer)

    initial = (
        jnp.full((heads_local, group * rows), masked, jnp.float32),
        jnp.zeros((heads_local, group * rows), jnp.float32),
        jnp.zeros((heads_local, group * rows, width), jnp.float32),
    )
    state = lax.fori_loop(0, key_total // span, visit_block, initial)
    ranks_local = page_ranks(owners)
    capacity = 2 * (rows // PAGE)
    empty = (
        jnp.zeros((heads_local, capacity, PAGE * 2 * width), jnp.float32),
        jnp.zeros((heads_local, capacity, 2), jnp.float32),
    )
    mine_values, mine_tops = quantize(own_rows, heads_local, width, PAGE)
    own_pages = mine_values.shape[1]
    my_targets = lax.dynamic_slice_in_dim(owners, myself * own_pages, own_pages, 1)
    address = (
        my_targets[None, :, :] == jnp.arange(owner_count, dtype=jnp.int32)[:, None, None]
    ).astype(jnp.bfloat16)
    outgoing_values = address[..., None] * mine_values[None]
    outgoing_tops = address[..., None] * mine_tops[None]
    arrived_values, arrived_tops = (
        lax.all_to_all(outgoing_values, "dec", split_axis=0, concat_axis=0, tiled=True),
        lax.all_to_all(outgoing_tops, "dec", split_axis=0, concat_axis=0, tiled=True),
    )
    arrived_values = arrived_values.transpose(1, 0, 2, 3).reshape(
        heads_local, owner_count * own_pages, PAGE * 2 * width
    )
    arrived_tops = arrived_tops.transpose(1, 0, 2, 3).reshape(
        heads_local, owner_count * own_pages, 2
    )
    filled = place_pages(empty, (arrived_values, arrived_tops), owners, ranks_local, myself)
    highest, mass, numer = state
    result = (numer / mass[..., None]).astype(jnp.bfloat16)
    result = (
        result.reshape(heads_local, group, rows, width)
        .transpose(2, 0, 1, 3)
        .reshape(1, rows, heads_local * group * width)
    )
    attention = lax.all_to_all(result, "seq", split_axis=1, concat_axis=2, tiled=True)
    stored = filled[0].astype(jnp.bfloat16).reshape(heads_local, 1, capacity, PAGE, 2 * width)
    scales = filled[1].astype(jnp.bfloat16).reshape(heads_local, 1, capacity, 2)
    return (attention, stored, scales)


def solution(mesh):
    return jax.shard_map(
        on_device,
        mesh=mesh,
        in_specs=(
            P(("rep", "dec"), "seq", None),
            P(("rep", "dec"), "seq", None),
            P(("rep", "dec"), "seq"),
            P(("rep", "seq"), None),
            P("rep"),
        ),
        out_specs=(
            P(("rep", "dec"), "seq", None),
            P(("rep", "seq"), "dec", None, None, None),
            P(("rep", "seq"), "dec", None, None),
        ),
        check_vma=False,
    )
```

profile of v0, /device:TPU:6, one launch (start us, length us, event | category | flops | bytes accessed | tf_op | source)
XLA Modules:
  0.0 324.2 jit_solution(157306615418579144)
XLA Ops:
  7.2 2.0 copy.120
  9.8 11.6 %reduce.17 = bf16[2048,16]{1,0:T(8,128)(2,1)S(1)} reduce(bf16[2048,1,16]{2,1,0:T(2,128)(2,1)S(1)} %bitcast.123, bf16[]{:T(256)} %broadcast.388), dimensions={1}, to_apply=%bitcast.85.reduce_sub_computation | reduce | bytes 131074
  21.3 1.2 reshape.662
  22.5 10.3 %all-to-all-start = ((bf16[8,2,2048]{2,1,0:T(2,128)(2,1)}), bf16[8,2,2048]{2,1,0:T(2,128)(2,1)}, u32[]{:S(2)}, u32[]{:S(2)}) async-start(bf16[8,2,2048]{2,1,0:T(2,128)(2,1)} %reshape.662), calls=%async_computation | async-start | bytes 131072 | tf_op jit(solution)/shard_map/all_to_all | solution.py:65
  33.5 49.9 %all_gather.6 = bf16[1024,256]{1,0:T(8,128)(2,1)S(1)} all-gather(bf16[32,256]{1,0:T(8,128)(2,1)S(1)} %copy-done.3), channel_id=1, replica_groups=mesh['seq'=8,'dec'=32,'rep'=2] {'dec'}, dimensions={0}, use_global_device_ids=true | all-gather | bytes 540672 | tf_op jit(solution)/shard_map/all_gather | solution.py:89
  84.8 6.7 %copy.129 = bf16[1,16,8192]{1,0,2:T(2,128)(2,1)} copy(bf16[1,16,8192]{2,1,0:T(8,128)(2,1)S(1)} %copy-done) | data formatting | bytes 524288 | tf_op args[0]
  91.4 45.3 %reduce.18 = bf16[8192,16]{1,0:T(8,128)(2,1)S(1)} reduce(bf16[8192,1,16]{2,1,0:T(2,128)(2,1)} %bitcast.120, bf16[]{:T(256)} %broadcast.388), dimensions={1}, to_apply=%bitcast.87.reduce_sub_computation | reduce | bytes 524290
  136.7 2.8 reshape.664
  140.2 0.7 compare_convert_fusion
  140.9 7.1 %all-to-all-start.1 = ((bf16[8,2,8192]{2,1,0:T(2,128)(2,1)}), bf16[8,2,8192]{2,1,0:T(2,128)(2,1)S(1)}, u32[]{:S(2)}, u32[]{:S(2)}) async-start(bf16[8,2,8192]{2,1,0:T(2,128)(2,1)} %reshape.664), calls=%async_computation.1 | async-start | bytes 524288 | tf_op jit(solution)/shard_map/all_to_all | solution.py:64
  148.3 2.1 reshape.663
  152.9 0.7 copy.139
  153.7 5.2 %broadcast_multiply_fusion = bf16[32,1,1,32768]{3,2,1,0:T(2,128)(2,1)} fusion(bf16[32768]{0:T(1024)(128)(2,1)S(1)} %bitcast.138, bf16[32]{0:T(256)(128)(2,1)S(1)} %compare_convert_fusion), kind=kLoop, calls=%fused_computation.34 | loop fusion | flops 1048576 | bytes 2162752 | tf_op jit(solution)/shard_map/mul | solution.py:144
  158.9 13.2 %reduce.20 = bf16[32,32768]{1,0:T(8,128)(2,1)S(1)} reduce(bf16[32,1,1,32768]{3,2,1,0:T(2,128)(2,1)} %broadcast_multiply_fusion, bf16[]{:T(256)} %broadcast.388), dimensions={1,2}, to_apply=%broadcast_multiply_fusion.reduce_sub_computation | reduce | bytes 4194306 | tf_op jit(solution)/shard_map/mul | solution.py:144
  172.1 2.8 reshape.668
  174.9 1.3 broadcast_multiply_fusion.1
  176.2 7.9 %all-to-all-start.4 = ((bf16[32,1,1,2]{3,2,1,0:T(2,128)(2,1)}), bf16[32,1,1,2]{3,2,1,0:T(2,128)(2,1)S(1)}, u32[]{:S(2)}, u32[]{:S(2)}) async-start(bf16[32,1,1,2]{3,2,1,0:T(2,128)(2,1)} %broadcast_multiply_fusion.1), calls=%async_computation.4 | async-start | bytes 32768 | tf_op jit(solution)/shard_map/all_to_all | solution.py:148
  184.1 5.1 %reshape.665 = bf16[8192,1,16]{2,1,0:T(2,128)(2,1)} reshape(bf16[8,2,8192]{2,1,0:T(2,128)(2,1)S(1)} %all-to-all-done.1) | data formatting | bytes 524288
  189.1 7.9 %copy.130 = bf16[1,16,8192]{2,1,0:T(8,128)(2,1)S(1)} copy(bf16[1,16,8192]{1,0,2:T(2,128)(2,1)} %bitcast.119) | data formatting | bytes 524288 | tf_op jit(solution)/shard_map/all_to_all | solution.py:64
  197.9 35.1 %all-gather.2.cloned.1.call-done = bf16[4096,256]{0,1:T(8,128)(2,1)} async-done(((bf16[128,256]{0,1:T(8,128)(2,1)}), bf16[4096,256]{0,1:T(8,128)(2,1)}) %all-gather.2.cloned.1.call-update) | async-done | bytes 2097168 | tf_op jit(solution)/shard_map/all_gather | solution.py:90
  232.9 3.3 %pad_maximum_fusion = bf16[5120,256]{0,1:T(8,128)(2,1)} fusion(bf16[4096,256]{0,1:T(8,128)(2,1)} %all-gather.2.cloned.1.call-done, bf16[1024,256]{0,1:T(8,128)(2,1)S(1)} %copy.128), kind=kLoop, calls=%fused_computation.31 | loop fusion | flops 5242880 | bytes 5242880 | tf_op jit(solution)/shard_map/concatenate | solution.py:92
  236.8 8.1 %all-to-all-start.3 = ((bf16[32,2,16384]{2,1,0:T(2,128)(2,1)}), bf16[32,2,16384]{2,1,0:T(2,128)(2,1)}, u32[]{:S(2)}, u32[]{:S(2)}) async-start(bf16[32,2,16384]{2,1,0:T(2,128)(2,1)} %reshape.668), calls=%async_computation.3 | async-start | bytes 4194304 | tf_op jit(solution)/shard_map/all_to_all | solution.py:147
  244.9 43.4 %while.20 = (s32[]{:T(128)}, f32[1,1024]{1,0:T(1,128)S(1)}, f32[1,1024]{1,0:T(1,128)S(1)}, f32[1,1024,128]{2,1,0:T(8,128)S(1)}, s32[]{:T(128)}, /*index=5*/bf16[...) while((s32[]{:T(128)}, f32[1,1024]{1,0:T(1,128)S(1)}, ...), condition=%wide.region_3.4_spmd.clone, body=%wide.region_0.3_spmd.clone.sunk | while | flops 276700672 | bytes 8483519 | solution.py:131
  245.0 1.0 constant_dynamic-slice_fusion.3
  246.6 0.8 fusion.57
  248.1 1.1 fusion.61
  249.3 1.0 constant_dynamic-slice_fusion.3
  251.0 0.8 fusion.57
  251.8 0.7 fusion.59
  252.5 1.1 fusion.61
  253.6 1.0 constant_dynamic-slice_fusion.3
  255.3 0.8 fusion.57
  256.8 1.1 fusion.61
  258.0 1.0 constant_dynamic-slice_fusion.3
  259.6 0.8 fusion.57
  261.2 1.1 fusion.61
  262.3 1.0 constant_dynamic-slice_fusion.3
  264.0 0.8 fusion.57
  264.8 0.7 fusion.59
  265.5 1.1 fusion.61
  266.7 1.0 constant_dynamic-slice_fusion.3
  268.3 0.8 fusion.57
  269.8 1.1 fusion.61
  271.0 1.0 constant_dynamic-slice_fusion.3
  272.7 0.8 fusion.57
  273.5 0.7 fusion.59
  274.2 1.1 fusion.61
  275.3 1.0 constant_dynamic-slice_fusion.3
  277.0 0.8 fusion.57
  277.8 0.7 fusion.59
  278.5 1.1 fusion.61
  279.7 1.0 constant_dynamic-slice_fusion.3
  281.3 0.8 fusion.57
  282.2 0.7 fusion.59
  282.9 1.1 fusion.61
  284.0 1.0 constant_dynamic-slice_fusion.3
  285.7 0.8 fusion.57
  287.2 1.1 fusion.61
  289.3 2.2 reduce.19
  291.5 0.9 reshape.666
  292.4 7.4 %all-to-all-start.2 = ((bf16[8,2,8192]{2,1,0:T(2,128)(2,1)}), bf16[8,2,8192]{2,1,0:T(2,128)(2,1)S(1)}, u32[]{:S(2)}, u32[]{:S(2)}) async-start(bf16[8,2,8192]{2,1,0:T(2,128)(2,1)} %reshape.666), calls=%async_computation.2 | async-start | bytes 524288 | tf_op jit(solution)/shard_map/all_to_all | solution.py:164
  300.7 10.4 %reshape.669 = bf16[32,1,1,32768]{3,2,1,0:T(2,128)(2,1)} reshape(bf16[32,2,16384]{2,1,0:T(2,128)(2,1)} %all-to-all-done.3) | data formatting | bytes 4194304
  311.1 4.5 %convolution_convert_fusion = bf16[2,32768]{1,0:T(2,128)(2,1)S(1)} fusion(bf16[32,1,1,32768]{3,2,1,0:T(2,128)(2,1)} %reshape.669, pred[32]{0:T(512)(128)(4,1)S(1)} %copy-done.8, s32[32]{0:T(128)S(1)} %convert_reduce_fusion), kind=kOutput, calls=%fused_computation.30 | convolution fusion | flops 4259968 | bytes 2228384 | tf_op jit(solution)/shard_map/gsj,gjc->gsc/dot_general | solution.py:57
  316.7 0.7 copy.145
  (138 shorter events, 19.9 us)
Async XLA Ops:
  7.2 26.4 %copy-start.3 = (bf16[32,256]{1,0:T(8,128)(2,1)S(1)}, bf16[32,256]{1,0:T(8,128)(2,1)}, u32[]{:S(2)}) copy-start(bf16[32,256]{1,0:T(8,128)(2,1)} %param.9) | copy-start | bytes 49156
  7.2 76.3 %copy-start.9 = (s32[1,32]{1,0:T(1,128)S(1)}, s32[1,32]{1,0:T(1,128)}, u32[]{:S(2)}) copy-start(s32[1,32]{1,0:T(1,128)} %param.10) | copy-start | bytes 388
  9.2 75.6 %copy-start = (bf16[1,16,8192]{2,1,0:T(8,128)(2,1)S(1)}, bf16[1,16,8192]{2,1,0:T(8,128)(2,1)}, u32[]{:S(2)}) copy-start(bf16[1,16,8192]{2,1,0:T(8,128)(2,1)} %param.7) | copy-start | bytes 786436
  22.5 118.4 %all-to-all-start = ((bf16[8,2,2048]{2,1,0:T(2,128)(2,1)}), bf16[8,2,2048]{2,1,0:T(2,128)(2,1)}, u32[]{:S(2)}, u32[]{:S(2)}) async-start(bf16[8,2,2048]{2,1,0:T(2,128)(2,1)} %reshape.662), calls=%async_computation | async-start | bytes 131072 | tf_op jit(solution)/shard_map/all_to_all | solution.py:65
  84.0 0.5 copy-start.4
  136.7 2.9 copy-start.10
  139.5 11.7 %copy-start.5 = (f32[128]{0:T(128)S(1)}, f32[128]{0:T(128)}, u32[]{:S(2)}) copy-start(f32[128]{0:T(128)} %copy-done.4) | copy-start | bytes 1540
  140.9 12.8 %copy-start.6 = (bf16[32]{0:T(256)(128)(2,1)}, bf16[32]{0:T(256)(128)(2,1)S(1)}, u32[]{:S(2)}) copy-start(bf16[32]{0:T(256)(128)(2,1)S(1)} %compare_convert_fusion) | copy-start | bytes 196
  140.9 35.2 %all-to-all-start.1 = ((bf16[8,2,8192]{2,1,0:T(2,128)(2,1)}), bf16[8,2,8192]{2,1,0:T(2,128)(2,1)S(1)}, u32[]{:S(2)}, u32[]{:S(2)}) async-start(bf16[8,2,8192]{2,1,0:T(2,128)(2,1)} %reshape.664), calls=%async_computation.1 | async-start | bytes 524288 | tf_op jit(solution)/shard_map/all_to_all | solution.py:64
  148.1 84.9 %all-gather.2.cloned.1.call-start = ((), (), s32[]{:S(2)}) async-start(), calls=%async_computation.5 | async-start | bytes 2162688 | tf_op jit(solution)/shard_map/all_gather | solution.py:90
  172.1 2.8 copy-start.7
  176.2 60.0 %all-to-all-start.4 = ((bf16[32,1,1,2]{3,2,1,0:T(2,128)(2,1)}), bf16[32,1,1,2]{3,2,1,0:T(2,128)(2,1)S(1)}, u32[]{:S(2)}, u32[]{:S(2)}) async-start(bf16[32,1,1,2]{3,2,1,0:T(2,128)(2,1)} %broadcast_multiply_fusion.1), calls=%async_computation.4 | async-start | bytes 32768 | tf_op jit(solution)/shard_map/all_to_all | solution.py:148
  236.2 0.6 copy-start.1
  236.8 55.6 %all-to-all-start.3 = ((bf16[32,2,16384]{2,1,0:T(2,128)(2,1)}), bf16[32,2,16384]{2,1,0:T(2,128)(2,1)}, u32[]{:S(2)}, u32[]{:S(2)}) async-start(bf16[32,2,16384]{2,1,0:T(2,128)(2,1)} %reshape.668), calls=%async_computation.3 | async-start | bytes 4194304 | tf_op jit(solution)/shard_map/all_to_all | solution.py:147
  288.4 11.4 %copy-start.11 = (s32[1,32]{1,0:T(1,128)S(1)}, s32[1,32]{1,0:T(1,128)}, u32[]{:S(2)}) copy-start(s32[1,32]{1,0:T(1,128)} %param.10) | copy-start | bytes 388
  288.4 11.6 %copy-start.2 = (bf16[32,1,1,2]{3,2,1,0:T(2,128)(2,1)S(1)}, bf16[32,1,1,2]{3,2,1,0:T(2,128)(2,1)}, u32[]{:S(2)}) copy-start(bf16[32,1,1,2]{3,2,1,0:T(2,128)(2,1)} %copy-done.1) | copy-start | bytes 388
  288.4 11.7 %copy-start.8 = (pred[32]{0:T(512)(128)(4,1)S(1)}, pred[32]{0:T(512)(128)(4,1)}, u32[]{:S(2)}) copy-start(pred[32]{0:T(512)(128)(4,1)} %compare_bitcast_fusion) | copy-start | bytes 100
  292.4 23.9 %all-to-all-start.2 = ((bf16[8,2,8192]{2,1,0:T(2,128)(2,1)}), bf16[8,2,8192]{2,1,0:T(2,128)(2,1)S(1)}, u32[]{:S(2)}, u32[]{:S(2)}) async-start(bf16[8,2,8192]{2,1,0:T(2,128)(2,1)} %reshape.666), calls=%async_computation.2 | async-start | bytes 524288 | tf_op jit(solution)/shard_map/all_to_all | solution.py:164
Sparse Core Ops, SparseCore 0:
  153.8 79.0 all-gather.1
where the time goes:
time: 326 us; the launch traced here: 324 us
  other arithmetic  99.3 us (30%)
  local copies, waits for them, and re-layouts  58.6 us (18%)
  blocking collectives  49.9 us (15%)
  starting transfers between devices  41.1 us (13%)
  waiting for transfers between devices  35.1 us (11%)
  matrix products  24.2 us (7%)
  between operations  15.1 us (5%)
    unnamed x6, other arithmetic  59 us
    all_gather x1, blocking collectives, on_device(): prefix_whole = lax.all_gather(prefix_kv, 'dec', axis=0, tiled=True)  49.9 us
    unnamed x40, local copies, waits for them, and re-layouts  36.5 us
    all_gather x1, waiting for transfers between devices, on_device(): slab_whole = lax.all_gather(own_rows, 'dec', axis=0, tiled=True)  35.1 us
    mul x2, other arithmetic, on_device(): outgoing_values = address[..., None] * mine_values[None]  18.3 us
    dot_general x10, matrix products, visit_block(): jnp.einsum('grn,ngd->grd', weights.astype(jnp.bfloat16), split_rows[:, :,...  11.3 us
    all_to_all x1, starting transfers between devices, on_device(): lax.all_to_all(slab_kv, 'seq', split_axis=2, concat_axis=1, tiled=True)  10.3 us
    dynamic_slice x10, local copies, waits for them, and re-layouts, visit_block(): block_rows = lax.dynamic_slice_in_dim(key_rows, first, span, 0)  9.73 us
  transfers between devices with their start and end apart: 6, of which 1 were waited for; matrix products, arithmetic and copies ran while one was open for 51% of the time, Pallas kernels for 0%

commit v1 on v0

v1 whole, which is shorter than its diff:
```python
import functools
import math

import jax
import jax.numpy as jnp
import numpy as np
from jax import lax
from jax.experimental import pallas as pl
from jax.experimental.pallas import tpu as pltpu
from jax.sharding import Mesh, PartitionSpec as P

HQ = 64
KVH = 8
HD = 128
PAGE = 128
GROUP = HQ // KVH
TOK = 16
WIDE = 2 * HD
NX = 4

rope_base = 1000000.0
tiny = 1e-06
masked = -1e30
to_exp2 = HD ** (-0.5) * math.log2(math.e)

VMEM = pltpu.VMEM
SMEM = pltpu.SMEM


def spec(space=VMEM):
    return pl.BlockSpec(memory_space=space)


def params(mib=48):
    return pltpu.CompilerParams(vmem_limit_bytes=mib * 1024 * 1024)


def turn(x, cosine, sinus):
    x = x.astype(jnp.float32)
    return (x * cosine + pltpu.roll(x, HD // 2, 1) * sinus).astype(jnp.bfloat16)


def pack_kv(pos_ref, inv_ref, kv_ref, out_ref, cos_ref, sin_ref):
    row = lax.broadcasted_iota(jnp.int32, (TOK, HD), 0) + pos_ref[0]
    angles = row.astype(jnp.float32) * inv_ref[...]
    lane = lax.broadcasted_iota(jnp.int32, (TOK, HD), 1)
    cosine = jnp.cos(angles)
    sinus = jnp.sin(angles)
    sinus = jnp.where(lane < HD // 2, -sinus, sinus)
    cos_ref[...] = cosine
    sin_ref[...] = sinus
    for h in range(KVH):
        key = turn(kv_ref[:, h * WIDE : h * WIDE + HD], cosine, sinus)
        value = kv_ref[:, h * WIDE + HD : (h + 1) * WIDE]
        for y in range(out_ref.shape[1]):
            out_ref[h, y, :, :HD] = key
            out_ref[h, y, :, HD:] = value


def pack_q(cos_ref, sin_ref, q_ref, out_ref):
    cosine = cos_ref[...]
    sinus = sin_ref[...]
    for q in range(HQ):
        h, g = divmod(q, GROUP)
        out_ref[h, :, g * HD : (g + 1) * HD] = turn(q_ref[:, q * HD : (q + 1) * HD], cosine, sinus)


def scores_of(q, k):
    return lax.dot_general(q, k, (((1,), (1,)), ((), ())), preferred_element_type=jnp.float32)


def lane_sum(p):
    total = p[:, :HD]
    for i in range(1, p.shape[1] // HD):
        total = total + p[:, i * HD : (i + 1) * HD]
    return total


def attend(q_ref, k, v, m_ref, l_ref, a_ref, mask=None, first=False):
    rows = PAGE
    for g in range(GROUP):
        part = slice(g * rows, (g + 1) * rows)
        s = scores_of(q_ref[part], k)
        if mask is not None:
            s = jnp.where(mask, s, masked)
        top = jnp.max(s, axis=1, keepdims=True)
        if first:
            high = jnp.broadcast_to(top, (rows, HD))
        else:
            before = m_ref[part]
            high = jnp.maximum(before, top)
            factor = jnp.exp2((before - high) * to_exp2)
        shift = high[:, :1] * to_exp2
        p = jnp.exp2(s * to_exp2 - shift)
        add = lane_sum(p)
        num = jnp.dot(p.astype(jnp.bfloat16), v, preferred_element_type=jnp.float32)
        m_ref[part] = high
        if first:
            l_ref[part] = add
            a_ref[part] = num
        else:
            l_ref[part] = l_ref[part] * factor + add
            a_ref[part] = a_ref[part] * factor + num


def fill_q(q_in, q_ref):
    for g in range(GROUP):
        q_ref[g * PAGE : (g + 1) * PAGE] = q_in[:, :, g * HD : (g + 1) * HD].reshape(PAGE, HD)


def attend_near(place_ref, q_in, col_ref, pre_ref, m_ref, l_ref, a_ref, q_ref):
    y, begin = place_ref[0], place_ref[2]
    fill_q(q_in, q_ref)

    def block(i):
        both = col_ref[:, i].reshape(PAGE, WIDE)
        return both[:, :HD], both[:, HD:]

    row = lax.broadcasted_iota(jnp.int32, (PAGE, PAGE), 0)
    key = lax.broadcasted_iota(jnp.int32, (PAGE, PAGE), 1)
    k, v = block(y)
    attend(q_ref, k, v, m_ref, l_ref, a_ref, mask=key <= row, first=True)

    @pl.loop(0, y)
    def _(i):
        k, v = block(i)
        attend(q_ref, k, v, m_ref, l_ref, a_ref)

    span = 512
    where = lax.broadcasted_iota(jnp.int32, (PAGE, span), 1)

    @pl.loop(0, pre_ref.shape[0] // span)
    def _(i):
        both = pre_ref[pl.ds(i * span, span), :]
        attend(q_ref, both[:, :HD], both[:, HD:], m_ref, l_ref, a_ref, mask=where + i * span < begin)


def attend_far(place_ref, q_in, all_ref, m_in, l_in, a_in, out_ref, m_ref, l_ref, a_ref, q_ref):
    y, x = place_ref[0], place_ref[1]
    fill_q(q_in, q_ref)
    m_ref[...] = m_in[...]
    l_ref[...] = l_in[...]
    a_ref[...] = a_in[...]
    columns = [(x + j) % NX for j in range(1, NX)]

    @pl.loop(0, y)
    def _(i):
        both = jnp.concatenate([all_ref[c, :, i].reshape(PAGE, WIDE) for c in columns], axis=0)
        attend(q_ref, both[:, :HD], both[:, HD:], m_ref, l_ref, a_ref)

    @pl.loop(0, x)
    def _(c):
        both = all_ref[c, :, y].reshape(PAGE, WIDE)
        attend(q_ref, both[:, :HD], both[:, HD:], m_ref, l_ref, a_ref)

    for g in range(GROUP):
        part = slice(g * PAGE, (g + 1) * PAGE)
        mass = jnp.sum(l_ref[part], axis=1, keepdims=True)
        done = (a_ref[part] / mass).astype(jnp.bfloat16)
        out_ref[:, :, g * HD : (g + 1) * HD] = done.reshape(KVH, TOK, HD)


def pick_pages(place_ref, own_ref, all_ref, store_ref, scale_ref):
    me = place_ref[0] * NX + place_ref[1]
    pages = own_ref.shape[1]

    def look(i, found):
        one, two = found
        p = pages - 1 - i
        hit = own_ref[0, p] == me
        return jnp.where(hit, p, one), jnp.where(hit, one, two)

    found = lax.fori_loop(0, pages, look, (jnp.int32(pages), jnp.int32(pages)))
    tops = []
    for slot in range(2):
        page = found[slot]
        held = (page < pages).astype(jnp.float32)
        page = jnp.minimum(page, pages - 1)
        both = all_ref[page % NX, :, page // NX].reshape(PAGE, WIDE).astype(jnp.float32)
        for half in range(2):
            part = both[:, half * HD : (half + 1) * HD]
            top = jnp.max(jnp.max(jnp.abs(part), axis=0, keepdims=True), axis=1, keepdims=True)
            store_ref[slot, :, half * HD : (half + 1) * HD] = (part / (top + tiny) * held).astype(jnp.bfloat16)
            tops.append(top * held)
    row = lax.broadcasted_iota(jnp.int32, (2, 2), 0)
    col = lax.broadcasted_iota(jnp.int32, (2, 2), 1)
    upper = jnp.where(col == 0, tops[0], tops[1])
    lower = jnp.where(col == 0, tops[2], tops[3])
    scale_ref[...] = jnp.where(row == 0, upper, lower).astype(jnp.bfloat16)


def unpack_out(in_ref, out_ref):
    for h in range(KVH):
        out_ref[:, h * GROUP * HD : (h + 1) * GROUP * HD] = in_ref[h]


def shaped(shape, dtype=jnp.bfloat16):
    return jax.ShapeDtypeStruct(shape, dtype)


def on_device(queries, slab_kv, prefix_kv, owners, offset):
    ny = lax.axis_size("y")
    y, x, s = lax.axis_index("y"), lax.axis_index("x"), lax.axis_index("seq")
    begin = offset[0]
    position = (begin + (y * NX + x) * PAGE + s * TOK).reshape(1)
    place = jnp.stack([y, x, begin]).astype(jnp.int32)
    half = np.arange(HD // 2, dtype=np.float64) * 2.0 / HD
    inverse = np.tile((rope_base ** (-half)).astype(np.float32), 2)[None]

    kv_send, cosine, sinus = pl.pallas_call(
        pack_kv,
        out_shape=(shaped((KVH, ny, TOK, WIDE)), shaped((TOK, HD), jnp.float32), shaped((TOK, HD), jnp.float32)),
        in_specs=[spec(SMEM), spec(), spec()],
        out_specs=(spec(), spec(), spec()),
        compiler_params=params(),
        name="pack_kv",
    )(position, jnp.asarray(inverse), slab_kv[0])
    column = lax.all_to_all(kv_send.reshape(KVH * ny, TOK, WIDE), ("seq", "y"), 0, 0, tiled=True)

    q_send = pl.pallas_call(
        pack_q,
        out_shape=shaped((KVH, TOK, GROUP * HD)),
        in_specs=[spec()] * 3,
        out_specs=spec(),
        compiler_params=params(),
        name="pack_q",
    )(cosine, sinus, queries[0])
    q_got = lax.all_to_all(q_send, "seq", 0, 0, tiled=True)

    pre_rows = prefix_kv.shape[0]
    pre_x = lax.all_to_all(jnp.broadcast_to(prefix_kv[None], (NX, pre_rows, WIDE)), "x", 0, 0, tiled=True)
    pre_x = pre_x.reshape(1, NX * pre_rows, WIDE)
    pre_all = lax.all_to_all(jnp.broadcast_to(pre_x, (ny, NX * pre_rows, WIDE)), "y", 0, 0, tiled=True)
    pre_all = pre_all.reshape(ny * NX * pre_rows, WIDE)

    every = lax.all_to_all(
        jnp.broadcast_to(column[None], (NX, KVH * ny, TOK, WIDE)), "x", 0, 0, tiled=True
    ).reshape(NX, KVH, ny, TOK, WIDE)

    rows = GROUP * PAGE
    state = (shaped((rows, HD), jnp.float32),) * 3
    keep = [VMEM((rows, HD), jnp.float32)] * 3
    hold_q = VMEM((rows, HD), jnp.bfloat16)
    m, l, a = pl.pallas_call(
        attend_near,
        out_shape=state,
        in_specs=[spec(SMEM), spec(), spec(), spec()],
        out_specs=(spec(),) * 3,
        scratch_shapes=[hold_q],
        compiler_params=params(),
        cost_estimate=pl.CostEstimate(flops=4 * rows * HD * 2048, bytes_accessed=3 << 20, transcendentals=rows * 2048),
        name="attend_near",
    )(place, q_got, column.reshape(KVH, ny, TOK, WIDE), pre_all)
    result = pl.pallas_call(
        attend_far,
        out_shape=shaped((KVH, TOK, GROUP * HD)),
        in_specs=[spec(SMEM)] + [spec()] * 5,
        out_specs=spec(),
        scratch_shapes=keep + [hold_q],
        compiler_params=params(),
        cost_estimate=pl.CostEstimate(flops=4 * rows * HD * 3072, bytes_accessed=4 << 20, transcendentals=rows * 3072),
        name="attend_far",
    )(place, q_got, every, m, l, a)
    out = lax.all_to_all(result, "seq", 0, 0, tiled=True)

    stored, scales = pl.pallas_call(
        pick_pages,
        out_shape=(shaped((2, PAGE, WIDE)), shaped((2, 2))),
        in_specs=[spec(SMEM), spec(SMEM), spec()],
        out_specs=(spec(), spec()),
        compiler_params=params(),
        name="pick_pages",
    )(place, owners, every)

    attention = pl.pallas_call(
        unpack_out,
        out_shape=shaped((TOK, HQ * HD)),
        in_specs=[spec()],
        out_specs=spec(),
        compiler_params=params(),
        name="unpack_out",
    )(out)
    return attention[None], stored[None, None], scales[None, None]


def solution(mesh):
    sizes = mesh.shape
    devices = mesh.devices.reshape(sizes["seq"], sizes["dec"] // NX, NX, sizes["rep"])
    whole = Mesh(devices, ("seq", "y", "x", "rep"))
    dec = ("y", "x")
    return jax.shard_map(
        on_device,
        mesh=whole,
        in_specs=(
            P(("rep",) + dec, "seq", None),
            P(("rep",) + dec, "seq", None),
            P(("rep",) + dec, "seq"),
            P(("rep", "seq"), None),
            P("rep"),
        ),
        out_specs=(
            P(("rep",) + dec, "seq", None),
            P(("rep", "seq"), dec, None, None, None),
            P(("rep", "seq"), dec, None, None),
        ),
        check_vma=False,
    )
```

time: 326 us -> 156 us (0.48)
  the two profiles are of different devices: /device:TPU:6 before, /device:TPU:62 now
where the time goes in v1:
time: 156 us; the launch traced here: 155 us
  blocking collectives  63.3 us (41%)
  Pallas kernels  57.2 us (37%)
  starting transfers between devices  13.2 us (8%)
  local copies, waits for them, and re-layouts  10.8 us (7%)
  waiting for transfers between devices  9.08 us (6%)
    pallas_call x1, Pallas kernels, on_device(): pl.pallas_call(attend_far, out_shape=shaped((KVH, TOK, GROUP * HD)), in_s...  28.5 us
    pallas_call x1, Pallas kernels, on_device(): pl.pallas_call(attend_near, out_shape=state, in_specs=[spec(SMEM), spec()...  26.1 us
    all_to_all x1, blocking collectives, on_device(): lax.all_to_all(kv_send.reshape(KVH * ny, TOK, WIDE), ('seq', 'y'), 0, 0,...  24.4 us
    all_to_all x1, blocking collectives, on_device(): q_got = lax.all_to_all(q_send, 'seq', 0, 0, tiled=True)  21.3 us
    all_to_all x1, blocking collectives, on_device(): lax.all_to_all(jnp.broadcast_to(pre_x, (ny, NX * pre_rows, WIDE)), 'y', 0...  17.6 us
    all_to_all x1, waiting for transfers between devices, on_device(): out = lax.all_to_all(result, 'seq', 0, 0, tiled=True)  8.92 us
    unnamed x20, local copies, waits for them, and re-layouts  7.95 us
    all_to_all x1, starting transfers between devices, on_device(): lax.all_to_all(jnp.broadcast_to(column[None], (NX, KVH * ny, TOK, WIDE)),...  4.9 us
  transfers between devices with their start and end apart: 3, of which 2 were waited for; matrix products, arithmetic and copies ran while one was open for 0% of the time, Pallas kernels for 18%

profile of v1, /device:TPU:62, one launch (start us, length us, event | category | flops | bytes accessed | tf_op | source)
XLA Modules:
  0.0 155.0 jit_solution(7827660294683967587)
XLA Ops:
  0.6 1.4 broadcast_in_dim.29
  2.0 4.8 %all-to-all-start.3 = ((bf16[4,32,256]{2,1,0:T(8,128)(2,1)}), bf16[4,32,256]{2,1,0:T(8,128)(2,1)S(1)}, u32[]{:S(2)}, u32[]{:S(2)}) async-start(bf16[4,32,256]{2,1,0:T(8,128)(2,1)} %broadcast_in_dim.29), calls=%async_computation.3 | async-start | bytes 131072 | tf_op jit(solution)/shard_map/all_to_all | solution.py:231
  7.4 0.0 copy-start.1
  7.4 0.8 copy-done.1
  8.3 0.0 copy-start.2
  8.3 0.7 copy-done.2
  8.9 0.1 pack_kv.1
  9.0 0.0 copy-start
  9.0 0.9 copy-done
  10.0 0.2 pack_q.1
  10.2 0.2 all-to-all-done.3
  10.3 21.3 %all_to_all.30.q_in = bf16[8,16,1024]{2,1,0:T(8,128)(2,1)S(1)} all-to-all(bf16[8,16,1024]{2,1,0:T(8,128)(2,1)S(1)} %pack_q.1), channel_id=1, replica_groups=mesh['seq'=8,'y'=8,'x'=4,'rep'=2] {'seq'}, dimensions={0} | all-to-all | bytes 524288 | tf_op jit(solution)/shard_map/all_to_all | solution.py:228
  31.6 17.6 %all_to_all.31 = bf16[8,128,256]{2,1,0:T(8,128)(2,1)S(1)} all-to-all(bf16[8,128,256]{2,1,0:T(8,128)(2,1)S(1)} %broadcast_in_dim.31), channel_id=1, replica_groups=mesh['seq'=8,'y'=8,'x'=4,'rep'=2] {'y'}, dimensions={0} | all-to-all | bytes 1048576 | tf_op jit(solution)/shard_map/all_to_all | solution.py:233
  49.3 24.4 %all_to_all.32 = bf16[64,16,256]{2,1,0:T(8,128)(2,1)S(1)} all-to-all(bf16[64,16,256]{2,1,0:T(8,128)(2,1)S(1)} %bitcast.18), channel_id=1, replica_groups=mesh['seq'=8,'y'=8,'x'=4,'rep'=2] {'seq','y'}, dimensions={0} | all-to-all | bytes 1048576 | tf_op jit(solution)/shard_map/all_to_all | solution.py:218
  73.7 1.5 broadcast_in_dim.28
  75.2 4.9 %all-to-all-start.2 = ((bf16[4,64,16,256]{3,2,1,0:T(8,128)(2,1)}), bf16[4,64,16,256]{3,2,1,0:T(8,128)(2,1)S(1)}, u32[]{:S(2)}, u32[]{:S(2)}) async-start(bf16[4,64,16,256]{3,2,1,0:T(8,128)(2,1)} %broadcast_in_dim.28), calls=%async_computation.2 | async-start | bytes 4194304 | tf_op jit(solution)/shard_map/all_to_all | solution.py:236
  80.1 0.1 pad_add_fusion.place_ref
  80.1 26.1 %attend_near.1 = (f32[1024,128]{1,0:T(8,128)S(1)}, f32[1024,128]{1,0:T(8,128)S(1)}, f32[1024,128]{1,0:T(8,128)S(1)}) custom-call(s32[3]{0:T(128)S(1)} %pad_add_fusion.place_ref, bf16[8,16,1024]{2,1,0:T(8,128)(2,1)S(1)} %all_to_all.30.q_in, bf16[8,8,16,256]{3,2,1,0:T(8,128)(2,1)S(1)} %bitcast.17, bf16[1024,256]{1,0:T(8,128)(2,1)S(1)} %bitcast.19), custom_call_target="tpu_custom_call" | custom-call | flops 1073741824 | bytes 3145728 | tf_op jit(solution)/shard_map/attend_near/pallas_call | solution.py:244
  106.3 0.0 copy-start.4
  106.3 0.8 copy-done.4
  107.1 0.0 copy-start.6
  107.1 0.8 copy-done.6
  107.9 0.0 copy-start.8
  107.9 0.8 copy-done.8
  108.7 0.0 all-to-all-done.2
  108.7 0.0 copy-start.5
  108.7 1.0 copy-done.5
  109.7 0.0 copy-start.7
  109.7 1.0 copy-done.7
  110.8 0.0 copy-start.9
  110.8 1.0 copy-done.9
  111.8 0.0 copy-start.3
  111.8 28.5 %attend_far.1 = bf16[8,16,1024]{2,1,0:T(8,128)(2,1)} custom-call(s32[3]{0:T(128)S(1)} %pad_add_fusion.place_ref, bf16[8,16,1024]{2,1,0:T(8,128)(2,1)S(1)} %all_to_all.30.q_in, bf16[4,8,8,16,256]{4,3,2,1,0:T(8,128)(2,1)S(1)} %bitcast.15, f32[1024,128]{1,0:T(8,128)S(1)} %copy-done.5, f32[1024,128]{1,0:T(8,128)S(1)} %copy-done.7, f32[1024,128]{1,0:T(8,128)S(1)} %copy-done.9), custom_call_target="tpu_custom_call" | custom-call | flops 1610612736 | bytes 4194304 | tf_op jit(solution)/shard_map/attend_far/pallas_call | solution.py:254
  140.3 3.5 %all-to-all-start.5 = ((bf16[8,16,1024]{2,1,0:T(8,128)(2,1)}), bf16[8,16,1024]{2,1,0:T(8,128)(2,1)S(1)}, u32[]{:S(2)}, u32[]{:S(2)}) async-start(bf16[8,16,1024]{2,1,0:T(8,128)(2,1)} %attend_far.1), calls=%async_computation.5 | async-start | bytes 524288 | tf_op jit(solution)/shard_map/all_to_all | solution.py:264
  143.8 0.0 copy-done.3
  143.8 1.6 %pick_pages.1 = (bf16[2,128,256]{2,1,0:T(8,128)(2,1)}, bf16[2,2]{1,0:T(2,128)(2,1)}) custom-call(s32[3]{0:T(128)S(1)} %pad_add_fusion.place_ref, s32[1,32]{1,0:T(1,128)S(1)} %copy-done.3, bf16[4,8,8,16,256]{4,3,2,1,0:T(8,128)(2,1)S(1)} %bitcast.16), custom_call_target="tpu_custom_call" | custom-call | tf_op jit(solution)/shard_map/pick_pages/pallas_call | solution.py:266
  145.4 8.9 %all-to-all-done.5.in_ref = bf16[8,16,1024]{2,1,0:T(8,128)(2,1)S(1)} async-done(((bf16[8,16,1024]{2,1,0:T(8,128)(2,1)}), bf16[8,16,1024]{2,1,0:T(8,128)(2,1)S(1)}, u32[]{:S(2)}, u32[]{:S(2)}) %all-to-all-start.5) | async-done | bytes 262176 | tf_op jit(solution)/shard_map/all_to_all | solution.py:264
  154.3 0.7 unpack_out.1
  (1 shorter events, 0.0 us)
Async XLA Ops:
  2.0 8.3 %all-to-all-start.3 = ((bf16[4,32,256]{2,1,0:T(8,128)(2,1)}), bf16[4,32,256]{2,1,0:T(8,128)(2,1)S(1)}, u32[]{:S(2)}, u32[]{:S(2)}) async-start(bf16[4,32,256]{2,1,0:T(8,128)(2,1)} %broadcast_in_dim.29), calls=%async_computation.3 | async-start | bytes 131072 | tf_op jit(solution)/shard_map/all_to_all | solution.py:231
  7.4 0.8 copy-start.1
  8.3 0.7 copy-start.2
  9.0 1.0 copy-start
  75.2 33.5 %all-to-all-start.2 = ((bf16[4,64,16,256]{3,2,1,0:T(8,128)(2,1)}), bf16[4,64,16,256]{3,2,1,0:T(8,128)(2,1)S(1)}, u32[]{:S(2)}, u32[]{:S(2)}) async-start(bf16[4,64,16,256]{3,2,1,0:T(8,128)(2,1)} %broadcast_in_dim.28), calls=%async_computation.2 | async-start | bytes 4194304 | tf_op jit(solution)/shard_map/all_to_all | solution.py:236
  106.3 0.8 copy-start.4
  107.1 0.8 copy-start.6
  107.9 0.8 copy-start.8
  108.7 1.0 copy-start.5
  109.7 1.0 copy-start.7
  110.8 1.0 copy-start.9
  111.8 32.0 %copy-start.3 = (s32[1,32]{1,0:T(1,128)S(1)}, s32[1,32]{1,0:T(1,128)}, u32[]{:S(2)}) copy-start(s32[1,32]{1,0:T(1,128)} %own_ref.1) | copy-start | bytes 388
  140.3 14.0 %all-to-all-start.5 = ((bf16[8,16,1024]{2,1,0:T(8,128)(2,1)}), bf16[8,16,1024]{2,1,0:T(8,128)(2,1)S(1)}, u32[]{:S(2)}, u32[]{:S(2)}) async-start(bf16[8,16,1024]{2,1,0:T(8,128)(2,1)} %attend_far.1), calls=%async_computation.5 | async-start | bytes 524288 | tf_op jit(solution)/shard_map/all_to_all | solution.py:264

commit v2 on v1

v2 whole, which is shorter than its diff:
```python
import math

import jax
import jax.numpy as jnp
import numpy as np
from jax import lax
from jax.experimental import pallas as pl
from jax.experimental.pallas import tpu as pltpu
from jax.sharding import Mesh, PartitionSpec as P

HQ = 64
KVH = 8
HD = 128
PAGE = 128
GROUP = HQ // KVH
TOK = 16
WIDE = 2 * HD
QW = GROUP * HD
ROWS = GROUP * PAGE
NX = 4
NY = 8
PRE = 32
SLAB = NY * PAGE
KEYS = SLAB + NY * PRE
SLOTS = 2
CHUNK = 512

rope_base = 1000000.0
tiny = 1e-06
masked = -1e30
to_exp2 = HD ** (-0.5) * math.log2(math.e)

VMEM = pltpu.VMEM
SMEM = pltpu.SMEM
f32 = jnp.float32
bf16 = jnp.bfloat16


def spec(space=VMEM):
    return pl.BlockSpec(memory_space=space)


def params(mib=48):
    return pltpu.CompilerParams(vmem_limit_bytes=mib * 1024 * 1024)


def cost(flops, moved, exps=0):
    return pl.CostEstimate(flops=flops, bytes_accessed=moved, transcendentals=exps)


def shaped(shape, dtype=bf16):
    return jax.ShapeDtypeStruct(shape, dtype)


def pack(pos_ref, inv_ref, q_ref, kv_ref, out_ref):
    row = lax.broadcasted_iota(jnp.int32, (TOK, HD), 0) + pos_ref[0]
    angles = row.astype(f32) * inv_ref[...]
    lane = lax.broadcasted_iota(jnp.int32, (TOK, HD), 1)
    cosine = jnp.cos(angles)
    sinus = jnp.sin(angles)
    sinus = jnp.where(lane < HD // 2, -sinus, sinus)

    def turn(x):
        x = x.astype(f32)
        return (x * cosine + pltpu.roll(x, HD // 2, 1) * sinus).astype(bf16)

    for h in range(KVH):
        for g in range(GROUP):
            q = h * GROUP + g
            out_ref[h, :, g * HD : (g + 1) * HD] = turn(q_ref[:, q * HD : (q + 1) * HD])
        out_ref[h, :, QW : QW + HD] = turn(kv_ref[:, h * WIDE : h * WIDE + HD])
        out_ref[h, :, QW + HD :] = kv_ref[:, h * WIDE + HD : (h + 1) * WIDE]


def spread(in_ref, pre_ref, kv_ref, q_ref):
    own = in_ref[:, :, QW:].reshape(PAGE, WIDE)
    pre = pre_ref[...]
    for j in range(NY):
        kv_ref[j, :PAGE] = own
        kv_ref[j, PAGE:] = pre
    for g in range(GROUP):
        q_ref[g * PAGE : (g + 1) * PAGE] = in_ref[:, :, g * HD : (g + 1) * HD].reshape(PAGE, HD)


def offer_pages(place_ref, own_ref, col_ref, out_ref):
    y, x = place_ref[0], place_ref[1]
    pages = own_ref.shape[1]
    lane = lax.broadcasted_iota(jnp.int32, (TOK, WIDE), 1)
    for dest in range(NX):
        me = y * NX + dest

        def look(i, found, me=me):
            one, two = found
            p = pages - 1 - i
            hit = own_ref[0, p] == me
            return jnp.where(hit, p, one), jnp.where(hit, one, two)

        found = lax.fori_loop(0, pages, look, (jnp.int32(pages), jnp.int32(pages)))
        for slot in range(SLOTS):
            page = found[slot]
            here = (page < pages) & (page % NX == x)
            at = slice(slot * PAGE, (slot + 1) * PAGE)
            top_at = slice(SLOTS * PAGE + slot * TOK, SLOTS * PAGE + (slot + 1) * TOK)

            @pl.when(here)
            def _(page=page, dest=dest, at=at, top_at=top_at):
                both = col_ref[page // NX, :PAGE, :].astype(f32)
                tops = []
                for half in range(2):
                    part = both[:, half * HD : (half + 1) * HD]
                    top = jnp.max(jnp.max(jnp.abs(part), axis=0, keepdims=True), axis=1, keepdims=True)
                    out_ref[dest, at, half * HD : (half + 1) * HD] = (part / (top + tiny)).astype(bf16)
                    tops.append(top)
                out_ref[dest, top_at, :] = jnp.where(lane < HD, tops[0], tops[1]).astype(bf16)

            @pl.when(jnp.logical_not(here))
            def _(dest=dest, at=at, top_at=top_at):
                out_ref[dest, at, :] = jnp.zeros((PAGE, WIDE), bf16)
                out_ref[dest, top_at, :] = jnp.zeros((TOK, WIDE), bf16)


def attend(place_ref, col_ref, q0_ref, q1_ref, q2_ref, q3_ref, out_ref, kt_ref, v_ref, s_ref, p_ref, l_ref, h_ref):
    y, x, begin = place_ref[0], place_ref[1], place_ref[2]
    queries = (q0_ref, q1_ref, q2_ref, q3_ref)
    for j in range(NY):
        b = (y + j) % NY
        kt_ref[:, j * PAGE : (j + 1) * PAGE] = col_ref[b, :PAGE, :HD].T
        v_ref[j * PAGE : (j + 1) * PAGE] = col_ref[b, :PAGE, HD:]
    kt_ref[:, SLAB:] = col_ref[:, PAGE:, :HD].reshape(NY * PRE, HD).T
    v_ref[SLAB:] = col_ref[:, PAGE:, HD:].reshape(NY * PRE, HD)

    c = lax.broadcasted_iota(jnp.int32, (1, KEYS), 1)
    b = (y + c // PAGE) % NY
    i = c - SLAB
    slab_bias = jnp.where((c < PAGE) | (b < y), 0.0, masked)
    prefix_bias = jnp.where(((i // PRE) * NX + x) * PRE + i % PRE < begin, 0.0, masked)
    bias = jnp.where(c < SLAB, slab_bias, prefix_bias)
    token = lax.broadcasted_iota(jnp.int32, (CHUNK, PAGE), 0) % PAGE
    own_key = lax.broadcasted_iota(jnp.int32, (CHUNK, PAGE), 1)
    lane = lax.broadcasted_iota(jnp.int32, (PAGE, HD), 1)
    per_set = ROWS // CHUNK
    total = NX * per_set

    def score(t):
        k, part = divmod(t, per_set)
        dest = (x + k) % NX
        reach = jnp.where(dest > x, PAGE, jnp.where(dest == x, 0, -PAGE))
        q = queries[k][part * CHUNK : (part + 1) * CHUNK]
        s = jnp.dot(q, kt_ref[...], preferred_element_type=f32) + bias
        at = slice(t % 2 * CHUNK, (t % 2 + 1) * CHUNK)
        s_ref[at, :PAGE] = jnp.where(own_key <= token + reach, s[:, :PAGE], masked)
        s_ref[at, PAGE:] = s[:, PAGE:]

    def weigh(t):
        at = slice(t % 2 * CHUNK, (t % 2 + 1) * CHUNK)
        s = s_ref[at, :]
        top = s[:, :HD]
        for n in range(1, KEYS // HD):
            top = jnp.maximum(top, s[:, n * HD : (n + 1) * HD])
        high = jnp.max(top, axis=1, keepdims=True) * to_exp2
        p = jnp.exp2(s * to_exp2 - high)
        mass = p[:, :HD]
        for n in range(1, KEYS // HD):
            mass = mass + p[:, n * HD : (n + 1) * HD]
        l_ref[at, :] = mass
        h_ref[at, :] = jnp.broadcast_to(high, (CHUNK, HD))
        p_ref[at, :] = p.astype(bf16)

    def gather(t, stats):
        k, part = divmod(t, per_set)
        dest = (x + k) % NX
        at = slice(t % 2 * CHUNK, (t % 2 + 1) * CHUNK)
        num = jnp.dot(p_ref[at, :], v_ref[...], preferred_element_type=f32)
        mass = jnp.sum(l_ref[at, :], axis=1, keepdims=True)
        out_ref[dest, part * CHUNK : (part + 1) * CHUNK] = (num / mass).astype(bf16)
        level = h_ref[at, :] + jnp.log2(mass)
        for g in range(CHUNK // PAGE):
            one = level[g * PAGE : (g + 1) * PAGE]
            for piece in range(3):
                rounded = one.astype(bf16).astype(f32)
                stats = jnp.where(lane == (part * (CHUNK // PAGE) + g) * 3 + piece, rounded, stats)
                one = one - rounded
        if part == per_set - 1:
            out_ref[dest, ROWS:] = stats.astype(bf16)
        return stats

    stats = None
    for t in range(total + 2):
        if t >= 2:
            if (t - 2) % per_set == 0:
                stats = jnp.zeros((PAGE, HD), f32)
            stats = gather(t - 2, stats)
        if t < total:
            score(t)
        if 1 <= t < total + 1:
            weigh(t - 1)


def combine(in_ref, out_ref):
    stats = [in_ref[i, ROWS:].astype(f32) for i in range(NX)]
    for g in range(GROUP):
        levels = [s[:, 3 * g : 3 * g + 1] + s[:, 3 * g + 1 : 3 * g + 2] + s[:, 3 * g + 2 : 3 * g + 3] for s in stats]
        top = jnp.maximum(jnp.maximum(levels[0], levels[1]), jnp.maximum(levels[2], levels[3]))
        shares = [jnp.exp2(v - top) for v in levels]
        whole = shares[0] + shares[1] + shares[2] + shares[3]
        done = jnp.zeros((PAGE, HD), f32)
        for i in range(NX):
            done = done + in_ref[i, g * PAGE : (g + 1) * PAGE].astype(f32) * (shares[i] / whole)
        out_ref[:, :, g * HD : (g + 1) * HD] = done.astype(bf16).reshape(KVH, TOK, HD)


def unpack(in_ref, out_ref):
    for h in range(KVH):
        out_ref[:, h * QW : (h + 1) * QW] = in_ref[h]


def keep_pages(in_ref, store_ref, scale_ref):
    for slot in range(SLOTS):
        store_ref[slot] = in_ref[slot * PAGE : (slot + 1) * PAGE]
    row = lax.broadcasted_iota(jnp.int32, (2, 2), 0)
    col = lax.broadcasted_iota(jnp.int32, (2, 2), 1)
    first = in_ref[SLOTS * PAGE : SLOTS * PAGE + TOK].astype(f32)
    second = in_ref[SLOTS * PAGE + TOK :].astype(f32)
    upper = jnp.where(col == 0, first[:1, :1], first[:1, HD : HD + 1])
    lower = jnp.where(col == 0, second[:1, :1], second[:1, HD : HD + 1])
    scale_ref[...] = jnp.where(row == 0, upper, lower).astype(bf16)


def on_device(queries, slab_kv, prefix_kv, owners, offset):
    y, x, s = lax.axis_index("y"), lax.axis_index("x"), lax.axis_index("seq")
    begin = offset[0]
    position = (begin + (y * NX + x) * PAGE + s * TOK).reshape(1)
    place = jnp.stack([y, x, begin]).astype(jnp.int32)
    half = np.arange(HD // 2, dtype=np.float64) * 2.0 / HD
    inverse = np.tile((rope_base ** (-half)).astype(np.float32), 2)[None]

    packed = pl.pallas_call(
        pack,
        out_shape=shaped((KVH, TOK, QW + WIDE)),
        in_specs=[spec(SMEM), spec(), spec(), spec()],
        out_specs=spec(),
        compiler_params=params(),
        name="pack",
    )(position, jnp.asarray(inverse), queries[0], slab_kv[0])
    grouped = lax.all_to_all(packed, "seq", 0, 0, tiled=True)

    kv_send, q_own = pl.pallas_call(
        spread,
        out_shape=(shaped((NY, PAGE + PRE, WIDE)), shaped((ROWS, HD))),
        in_specs=[spec(), spec()],
        out_specs=(spec(), spec()),
        compiler_params=params(),
        name="spread",
    )(grouped, prefix_kv)
    column = lax.all_to_all(kv_send, "y", 0, 0, tiled=True)
    asked = [q_own] + [lax.ppermute(q_own, "x", [(i, (i - k) % NX) for i in range(NX)]) for k in range(1, NX)]

    offered = pl.pallas_call(
        offer_pages,
        out_shape=shaped((NX, SLOTS * (PAGE + TOK), WIDE)),
        in_specs=[spec(SMEM), spec(SMEM), spec()],
        out_specs=spec(),
        compiler_params=params(),
        name="offer_pages",
    )(place, owners, column)
    delivered = lax.psum_scatter(
        offered.reshape(NX * SLOTS * (PAGE + TOK), WIDE), "x", scatter_dimension=0, tiled=True
    )

    parts = pl.pallas_call(
        attend,
        out_shape=shaped((NX, ROWS + PAGE, HD)),
        in_specs=[spec(SMEM)] + [spec()] * 5,
        out_specs=spec(),
        scratch_shapes=[
            VMEM((HD, KEYS), bf16),
            VMEM((KEYS, HD), bf16),
            VMEM((2 * CHUNK, KEYS), f32),
            VMEM((2 * CHUNK, KEYS), bf16),
            VMEM((2 * CHUNK, HD), f32),
            VMEM((2 * CHUNK, HD), f32),
        ],
        compiler_params=params(),
        cost_estimate=cost(4 * NX * ROWS * KEYS * HD, 4 << 20, NX * ROWS * KEYS),
        name="attend",
    )(place, column, *asked)
    parts = lax.all_to_all(parts, "x", 0, 0, tiled=True)
    result = pl.pallas_call(
        combine,
        out_shape=shaped((KVH, TOK, QW)),
        in_specs=[spec()],
        out_specs=spec(),
        compiler_params=params(),
        name="combine",
    )(parts)
    back = lax.all_to_all(result, "seq", 0, 0, tiled=True)
    attention = pl.pallas_call(
        unpack,
        out_shape=shaped((TOK, HQ * HD)),
        in_specs=[spec()],
        out_specs=spec(),
        compiler_params=params(),
        name="unpack",
    )(back)
    stored, scales = pl.pallas_call(
        keep_pages,
        out_shape=(shaped((SLOTS, PAGE, WIDE)), shaped((2, 2))),
        in_specs=[spec()],
        out_specs=(spec(), spec()),
        compiler_params=params(),
        name="keep_pages",
    )(delivered)
    return attention[None], stored[None, None], scales[None, None]


def solution(mesh):
    sizes = mesh.shape
    devices = mesh.devices.reshape(sizes["seq"], NY, NX, sizes["rep"])
    whole = Mesh(devices, ("seq", "y", "x", "rep"))
    dec = ("y", "x")
    return jax.shard_map(
        on_device,
        mesh=whole,
        in_specs=(
            P(("rep",) + dec, "seq", None),
            P(("rep",) + dec, "seq", None),
            P(("rep",) + dec, "seq"),
            P(("rep", "seq"), None),
            P("rep"),
        ),
        out_specs=(
            P(("rep",) + dec, "seq", None),
            P(("rep", "seq"), dec, None, None, None),
            P(("rep", "seq"), dec, None, None),
        ),
        check_vma=False,
    )
```

time: 156 us -> 114 us (0.73)
  the two profiles are of different devices: /device:TPU:62 before, /device:TPU:6 now
where the time goes in v2:
time: 114 us; the launch traced here: 112 us
  waiting for transfers between devices  28.5 us (25%)
  starting transfers between devices  26.7 us (23%)
  blocking collectives  23.4 us (21%)
  Pallas kernels  15.8 us (14%)
  between operations  14.7 us (13%)
  local copies, waits for them, and re-layouts  3.35 us (3%)
    all_to_all x1, blocking collectives, on_device(): grouped = lax.all_to_all(packed, 'seq', 0, 0, tiled=True)  23.4 us
    all_to_all x1, waiting for transfers between devices, on_device(): parts = lax.all_to_all(parts, 'x', 0, 0, tiled=True)  9.41 us
    pallas_call x1, Pallas kernels, on_device(): pl.pallas_call(attend, out_shape=shaped((NX, ROWS + PAGE, HD)), in_specs=...  9.34 us
    ppermute x3, waiting for transfers between devices, on_device(): lax.ppermute(q_own, 'x', [(i, (i - k) % NX) for i in range(NX)])  9.04 us
    ppermute x3, starting transfers between devices, on_device(): lax.ppermute(q_own, 'x', [(i, (i - k) % NX) for i in range(NX)])  8.62 us
    all_to_all x1, starting transfers between devices, on_device(): column = lax.all_to_all(kv_send, 'y', 0, 0, tiled=True)  7.1 us
    all_to_all x1, starting transfers between devices, on_device(): back = lax.all_to_all(result, 'seq', 0, 0, tiled=True)  6.02 us
    reduce_scatter x1, waiting for transfers between devices, on_device(): lax.psum_scatter(offered.reshape(NX * SLOTS * (PAGE + TOK), WIDE), 'x', s...  5.79 us
  transfers between devices with their start and end apart: 7, of which 7 were waited for; matrix products, arithmetic and copies ran while one was open for 0% of the time, Pallas kernels for 4%

profile of v2, /device:TPU:6, one launch (start us, length us, event | category | flops | bytes accessed | tf_op | source)
XLA Modules:
  0.0 112.5 jit_solution(3035595999832705672)
XLA Ops:
  7.2 0.0 copy-start.3
  7.8 0.0 copy-start
  7.9 0.9 copy-done
  8.8 0.0 copy-start.2
  8.8 0.8 copy-done.2
  9.6 0.0 copy-start.5
  9.6 0.7 copy-done.5
  10.3 0.2 pack.1
  10.5 23.4 %all_to_all.20.in_ref = bf16[8,16,1280]{2,1,0:T(8,128)(2,1)S(1)} all-to-all(bf16[8,16,1280]{2,1,0:T(8,128)(2,1)S(1)} %pack.1), channel_id=1, replica_groups=mesh['seq'=8,'y'=8,'x'=4,'rep'=2] {'seq'}, dimensions={0} | all-to-all | bytes 655360 | tf_op jit(solution)/shard_map/all_to_all | solution.py:245
  33.9 0.0 copy-done.3
  33.9 0.9 spread.1
  34.8 7.1 %all-to-all-start.1 = ((bf16[8,160,256]{2,1,0:T(8,128)(2,1)}), bf16[8,160,256]{2,1,0:T(8,128)(2,1)S(1)}, u32[]{:S(2)}, u32[]{:S(2)}) async-start(bf16[8,160,256]{2,1,0:T(8,128)(2,1)} %get-tuple-element.7), calls=%async_computation.1 | async-start | bytes 1310720 | tf_op jit(solution)/shard_map/all_to_all | solution.py:255
  41.9 2.4 %collective-permute-start.2 = (bf16[1024,128]{1,0:T(8,128)(2,1)S(1)}, bf16[1024,128]{1,0:T(8,128)(2,1)S(1)}, u32[]{:S(2)}, u32[]{:S(2)}) collective-permute-start(bf16[1024,128]{1,0:T(8,128)(2,1)S(1)} %get-tuple-element.8.q0_ref), channel_id=1, source_target_pairs={{0,2},{2,4},{4,6},{6,0},{1,3},{3,5},{5,7},{7,1},{8,10},{10,12},{12... | collective-permute-start | bytes 786440 | tf_op jit(solution)/shard_map/ppermute | solution.py:256
  44.3 4.3 %collective-permute-start.1 = (bf16[1024,128]{1,0:T(8,128)(2,1)S(1)}, bf16[1024,128]{1,0:T(8,128)(2,1)S(1)}, u32[]{:S(2)}, u32[]{:S(2)}) collective-permute-start(bf16[1024,128]{1,0:T(8,128)(2,1)S(1)} %get-tuple-element.8.q0_ref), channel_id=1, source_target_pairs={{0,4},{2,6},{4,0},{6,2},{1,5},{3,7},{5,1},{7,3},{8,12},{10,14},{12... | collective-permute-start | bytes 786440 | tf_op jit(solution)/shard_map/ppermute | solution.py:256
  48.6 1.9 %collective-permute-start = (bf16[1024,128]{1,0:T(8,128)(2,1)S(1)}, bf16[1024,128]{1,0:T(8,128)(2,1)S(1)}, u32[]{:S(2)}, u32[]{:S(2)}) collective-permute-start(bf16[1024,128]{1,0:T(8,128)(2,1)S(1)} %get-tuple-element.8.q0_ref), channel_id=1, source_target_pairs={{0,6},{2,0},{4,2},{6,4},{1,7},{3,1},{5,3},{7,5},{8,14},{10,8},{12,... | collective-permute-start | bytes 786440 | tf_op jit(solution)/shard_map/ppermute | solution.py:256
  50.5 0.1 pad_add_fusion.place_ref
  50.6 1.8 %collective-permute-done.2.q3_ref = bf16[1024,128]{1,0:T(8,128)(2,1)S(1)} collective-permute-done((bf16[1024,128]{1,0:T(8,128)(2,1)S(1)}, bf16[1024,128]{1,0:T(8,128)(2,1)S(1)}, u32[]{:S(2)}, u32[]{:S(2)}) %collective-permute-start.2) | collective-permute-done | bytes 262176 | tf_op jit(solution)/shard_map/ppermute | solution.py:256
  52.5 4.2 %collective-permute-done.1.q2_ref = bf16[1024,128]{1,0:T(8,128)(2,1)S(1)} collective-permute-done((bf16[1024,128]{1,0:T(8,128)(2,1)S(1)}, bf16[1024,128]{1,0:T(8,128)(2,1)S(1)}, u32[]{:S(2)}, u32[]{:S(2)}) %collective-permute-start.1) | collective-permute-done | bytes 262176 | tf_op jit(solution)/shard_map/ppermute | solution.py:256
  56.7 3.0 %collective-permute-done.q1_ref = bf16[1024,128]{1,0:T(8,128)(2,1)S(1)} collective-permute-done((bf16[1024,128]{1,0:T(8,128)(2,1)S(1)}, bf16[1024,128]{1,0:T(8,128)(2,1)S(1)}, u32[]{:S(2)}, u32[]{:S(2)}) %collective-permute-start) | collective-permute-done | bytes 262176 | tf_op jit(solution)/shard_map/ppermute | solution.py:256
  59.7 0.7 all-to-all-done.1.col_ref
  60.4 9.3 %attend.1 = bf16[4,1152,128]{2,1,0:T(8,128)(2,1)} custom-call(s32[3]{0:T(128)S(1)} %pad_add_fusion.place_ref, bf16[8,160,256]{2,1,0:T(8,128)(2,1)S(1)} %all-to-all-done.1.col_ref, bf16[1024,128]{1,0:T(8,128)(2,1)S(1)} %get-tuple-element.8.q0_ref, bf16[1024,128]{1,0:T(8,128)(2,1)S(1)} %collective-permute-done.q1_ref, ...), custom_call_target="tpu_custom_call" | custom-call | flops 2684354560 | bytes 4194304 | tf_op jit(solution)/shard_map/attend/pallas_call | solution.py:270
  69.7 0.0 copy-start.4
  69.7 4.9 %all-to-all-start.2 = ((bf16[4,1152,128]{2,1,0:T(8,128)(2,1)}), bf16[4,1152,128]{2,1,0:T(8,128)(2,1)S(1)}, u32[]{:S(2)}, u32[]{:S(2)}) async-start(bf16[4,1152,128]{2,1,0:T(8,128)(2,1)} %attend.1), calls=%async_computation.2 | async-start | bytes 2359296 | tf_op jit(solution)/shard_map/all_to_all | solution.py:287
  74.6 0.0 reduce-scatter.2.cloned.1.call-start
  74.6 0.0 copy-done.4
  74.6 2.4 %offer_pages.1 = bf16[4,288,256]{2,1,0:T(8,128)(2,1)} custom-call(s32[3]{0:T(128)S(1)} %pad_add_fusion.place_ref, s32[1,32]{1,0:T(1,128)S(1)} %copy-done.4, bf16[8,160,256]{2,1,0:T(8,128)(2,1)S(1)} %all-to-all-done.1.col_ref), custom_call_target="tpu_custom_call" | custom-call | tf_op jit(solution)/shard_map/offer_pages/pallas_call | solution.py:258
  77.0 0.0 reduce-scatter.2.cloned.1.call-update
  77.1 9.4 %all-to-all-done.2.in_ref = bf16[4,1152,128]{2,1,0:T(8,128)(2,1)S(1)} async-done(((bf16[4,1152,128]{2,1,0:T(8,128)(2,1)}), bf16[4,1152,128]{2,1,0:T(8,128)(2,1)S(1)}, u32[]{:S(2)}, u32[]{:S(2)}) %all-to-all-start.2) | async-done | bytes 1179680 | tf_op jit(solution)/shard_map/all_to_all | solution.py:287
  86.5 1.5 %combine.1 = bf16[8,16,1024]{2,1,0:T(8,128)(2,1)} custom-call(bf16[4,1152,128]{2,1,0:T(8,128)(2,1)S(1)} %all-to-all-done.2.in_ref), custom_call_target="tpu_custom_call" | custom-call | tf_op jit(solution)/shard_map/combine/pallas_call | solution.py:288
  88.0 6.0 %all-to-all-start.3 = ((bf16[8,16,1024]{2,1,0:T(8,128)(2,1)}), bf16[8,16,1024]{2,1,0:T(8,128)(2,1)S(1)}, u32[]{:S(2)}, u32[]{:S(2)}) async-start(bf16[8,16,1024]{2,1,0:T(8,128)(2,1)} %combine.1), calls=%async_computation.3 | async-start | bytes 524288 | tf_op jit(solution)/shard_map/all_to_all | solution.py:296
  94.0 5.8 %reduce-scatter.2.cloned.1.call-done.in_ref = bf16[288,256]{1,0:T(8,128)(2,1)} async-done(((bf16[1152,256]{1,0:T(8,128)(2,1)}), bf16[288,256]{1,0:T(8,128)(2,1)}) %reduce-scatter.2.cloned.1.call-update) | async-done | bytes 147472 | tf_op jit(solution)/shard_map/reduce_scatter | solution.py:266
  99.8 0.0 copy-start.1
  99.8 0.9 copy-done.1
  100.7 0.7 keep_pages.1
  101.4 3.5 %all-to-all-done.3.in_ref = bf16[8,16,1024]{2,1,0:T(8,128)(2,1)S(1)} async-done(((bf16[8,16,1024]{2,1,0:T(8,128)(2,1)}), bf16[8,16,1024]{2,1,0:T(8,128)(2,1)S(1)}, u32[]{:S(2)}, u32[]{:S(2)}) %all-to-all-start.3) | async-done | bytes 262176 | tf_op jit(solution)/shard_map/all_to_all | solution.py:296
  104.9 0.7 unpack.1
Async XLA Ops:
  7.2 26.7 %copy-start.3 = (bf16[32,256]{1,0:T(8,128)(2,1)S(1)}, bf16[32,256]{1,0:T(8,128)(2,1)}, u32[]{:S(2)}) copy-start(bf16[32,256]{1,0:T(8,128)(2,1)} %pre_ref.1) | copy-start | bytes 49156
  7.8 1.0 copy-start
  8.8 0.8 copy-start.2
  9.6 0.7 copy-start.5
  34.8 25.6 %all-to-all-start.1 = ((bf16[8,160,256]{2,1,0:T(8,128)(2,1)}), bf16[8,160,256]{2,1,0:T(8,128)(2,1)S(1)}, u32[]{:S(2)}, u32[]{:S(2)}) async-start(bf16[8,160,256]{2,1,0:T(8,128)(2,1)} %get-tuple-element.7), calls=%async_computation.1 | async-start | bytes 1310720 | tf_op jit(solution)/shard_map/all_to_all | solution.py:255
  41.9 10.6 %collective-permute-start.2 = (bf16[1024,128]{1,0:T(8,128)(2,1)S(1)}, bf16[1024,128]{1,0:T(8,128)(2,1)S(1)}, u32[]{:S(2)}, u32[]{:S(2)}) collective-permute-start(bf16[1024,128]{1,0:T(8,128)(2,1)S(1)} %get-tuple-element.8.q0_ref), channel_id=1, source_target_pairs={{0,2},{2,4},{4,6},{6,0},{1,3},{3,5},{5,7},{7,1},{8,10},{10,12},{12... | collective-permute-start | bytes 786440 | tf_op jit(solution)/shard_map/ppermute | solution.py:256
  44.3 12.4 %collective-permute-start.1 = (bf16[1024,128]{1,0:T(8,128)(2,1)S(1)}, bf16[1024,128]{1,0:T(8,128)(2,1)S(1)}, u32[]{:S(2)}, u32[]{:S(2)}) collective-permute-start(bf16[1024,128]{1,0:T(8,128)(2,1)S(1)} %get-tuple-element.8.q0_ref), channel_id=1, source_target_pairs={{0,4},{2,6},{4,0},{6,2},{1,5},{3,7},{5,1},{7,3},{8,12},{10,14},{12... | collective-permute-start | bytes 786440 | tf_op jit(solution)/shard_map/ppermute | solution.py:256
  48.6 11.1 %collective-permute-start = (bf16[1024,128]{1,0:T(8,128)(2,1)S(1)}, bf16[1024,128]{1,0:T(8,128)(2,1)S(1)}, u32[]{:S(2)}, u32[]{:S(2)}) collective-permute-start(bf16[1024,128]{1,0:T(8,128)(2,1)S(1)} %get-tuple-element.8.q0_ref), channel_id=1, source_target_pairs={{0,6},{2,0},{4,2},{6,4},{1,7},{3,1},{5,3},{7,5},{8,14},{10,8},{12,... | collective-permute-start | bytes 786440 | tf_op jit(solution)/shard_map/ppermute | solution.py:256
  69.7 4.9 %copy-start.4 = (s32[1,32]{1,0:T(1,128)S(1)}, s32[1,32]{1,0:T(1,128)}, u32[]{:S(2)}) copy-start(s32[1,32]{1,0:T(1,128)} %own_ref.1) | copy-start | bytes 388
  69.7 16.8 %all-to-all-start.2 = ((bf16[4,1152,128]{2,1,0:T(8,128)(2,1)}), bf16[4,1152,128]{2,1,0:T(8,128)(2,1)S(1)}, u32[]{:S(2)}, u32[]{:S(2)}) async-start(bf16[4,1152,128]{2,1,0:T(8,128)(2,1)} %attend.1), calls=%async_computation.2 | async-start | bytes 2359296 | tf_op jit(solution)/shard_map/all_to_all | solution.py:287
  74.6 25.2 %reduce-scatter.2.cloned.1.call-start = ((), (), s32[]{:S(2)}) async-start(), calls=%async_computation.5 | async-start | bytes 737280 | tf_op jit(solution)/shard_map/reduce_scatter | solution.py:266
  88.0 16.9 %all-to-all-start.3 = ((bf16[8,16,1024]{2,1,0:T(8,128)(2,1)}), bf16[8,16,1024]{2,1,0:T(8,128)(2,1)S(1)}, u32[]{:S(2)}, u32[]{:S(2)}) async-start(bf16[8,16,1024]{2,1,0:T(8,128)(2,1)} %combine.1), calls=%async_computation.3 | async-start | bytes 524288 | tf_op jit(solution)/shard_map/all_to_all | solution.py:296
  99.8 0.9 copy-start.1
Sparse Core Ops, SparseCore 0:
  78.3 21.4 reduce-scatter.1

commit v3 on v2

--- a/solution.py
+++ b/solution.py
@@ -24,6 +24,7 @@
 KEYS = SLAB + NY * PRE
 SLOTS = 2
 CHUNK = 512
+TOPS = ROWS + PAGE + SLOTS * 2 * PAGE
 
 rope_base = 1000000.0
 tiny = 1e-06
@@ -52,24 +53,36 @@
     return jax.ShapeDtypeStruct(shape, dtype)
 
 
-def pack(pos_ref, inv_ref, q_ref, kv_ref, out_ref):
+def pack(pos_ref, q_hbm, kv_hbm, out_ref, q_ref, kv_ref, sems):
+    fetch_q = pltpu.make_async_copy(q_hbm, q_ref, sems.at[0])
+    fetch_kv = pltpu.make_async_copy(kv_hbm, kv_ref, sems.at[1])
+    fetch_q.start()
+    fetch_kv.start()
+    half = HD // 2
+    lane = lax.broadcasted_iota(jnp.int32, (TOK, HD), 1)
+    place = lane % half
+    inverse = jnp.zeros((TOK, HD), f32)
+    for k in range(half):
+        inverse = jnp.where(place == k, float(np.float32(rope_base ** (-2.0 * k / HD))), inverse)
     row = lax.broadcasted_iota(jnp.int32, (TOK, HD), 0) + pos_ref[0]
-    angles = row.astype(f32) * inv_ref[...]
-    lane = lax.broadcasted_iota(jnp.int32, (TOK, HD), 1)
+    angles = row.astype(f32) * inverse
     cosine = jnp.cos(angles)
     sinus = jnp.sin(angles)
-    sinus = jnp.where(lane < HD // 2, -sinus, sinus)
+    sinus = jnp.where(lane < half, -sinus, sinus)
 
     def turn(x):
         x = x.astype(f32)
-        return (x * cosine + pltpu.roll(x, HD // 2, 1) * sinus).astype(bf16)
-
+        return (x * cosine + pltpu.roll(x, half, 1) * sinus).astype(bf16)
+
+    fetch_kv.wait()
+    for h in range(KVH):
+        out_ref[h, :, QW : QW + HD] = turn(kv_ref[:, h * WIDE : h * WIDE + HD])
+        out_ref[h, :, QW + HD :] = kv_ref[:, h * WIDE + HD : (h + 1) * WIDE]
+    fetch_q.wait()
     for h in range(KVH):
         for g in range(GROUP):
             q = h * GROUP + g
             out_ref[h, :, g * HD : (g + 1) * HD] = turn(q_ref[:, q * HD : (q + 1) * HD])
-        out_ref[h, :, QW : QW + HD] = turn(kv_ref[:, h * WIDE : h * WIDE + HD])
-        out_ref[h, :, QW + HD :] = kv_ref[:, h * WIDE + HD : (h + 1) * WIDE]
 
 
 def spread(in_ref, pre_ref, kv_ref, q_ref):
@@ -82,44 +95,31 @@
         q_ref[g * PAGE : (g + 1) * PAGE] = in_ref[:, :, g * HD : (g + 1) * HD].reshape(PAGE, HD)
 
 
-def offer_pages(place_ref, own_ref, col_ref, out_ref):
-    y, x = place_ref[0], place_ref[1]
+def offer_pages(x, y, own_ref, col_ref, out_ref):
     pages = own_ref.shape[1]
-    lane = lax.broadcasted_iota(jnp.int32, (TOK, WIDE), 1)
-    for dest in range(NX):
-        me = y * NX + dest
-
-        def look(i, found, me=me):
-            one, two = found
-            p = pages - 1 - i
-            hit = own_ref[0, p] == me
-            return jnp.where(hit, p, one), jnp.where(hit, one, two)
-
-        found = lax.fori_loop(0, pages, look, (jnp.int32(pages), jnp.int32(pages)))
+    found = [[jnp.int32(pages)] * SLOTS for _ in range(NX)]
+    for p in reversed(range(pages)):
+        dest = own_ref[0, p] - y * NX
+        for d in range(NX):
+            one, two = found[d]
+            found[d] = [jnp.where(dest == d, p, one), jnp.where(dest == d, one, two)]
+    tops = []
+    for d in range(NX):
+        tops.append([])
         for slot in range(SLOTS):
-            page = found[slot]
-            here = (page < pages) & (page % NX == x)
-            at = slice(slot * PAGE, (slot + 1) * PAGE)
-            top_at = slice(SLOTS * PAGE + slot * TOK, SLOTS * PAGE + (slot + 1) * TOK)
-
-            @pl.when(here)
-            def _(page=page, dest=dest, at=at, top_at=top_at):
-                both = col_ref[page // NX, :PAGE, :].astype(f32)
-                tops = []
-                for half in range(2):
-                    part = both[:, half * HD : (half + 1) * HD]
-                    top = jnp.max(jnp.max(jnp.abs(part), axis=0, keepdims=True), axis=1, keepdims=True)
-                    out_ref[dest, at, half * HD : (half + 1) * HD] = (part / (top + tiny)).astype(bf16)
-                    tops.append(top)
-                out_ref[dest, top_at, :] = jnp.where(lane < HD, tops[0], tops[1]).astype(bf16)
-
-            @pl.when(jnp.logical_not(here))
-            def _(dest=dest, at=at, top_at=top_at):
-                out_ref[dest, at, :] = jnp.zeros((PAGE, WIDE), bf16)
-                out_ref[dest, top_at, :] = jnp.zeros((TOK, WIDE), bf16)
-
-
-def attend(place_ref, col_ref, q0_ref, q1_ref, q2_ref, q3_ref, out_ref, kt_ref, v_ref, s_ref, p_ref, l_ref, h_ref):
+            page = found[d][slot]
+            held = jnp.where((page < pages) & (page % NX == x), 1.0, 0.0)
+            row = jnp.minimum(page // NX, NY - 1)
+            for half in range(2):
+                part = col_ref[row, :PAGE, half * HD : (half + 1) * HD].astype(f32)
+                top = jnp.max(jnp.max(jnp.abs(part), axis=0, keepdims=True), axis=1, keepdims=True)
+                at = ROWS + PAGE + (slot * 2 + half) * PAGE
+                out_ref[d, at : at + PAGE] = (part * (held / (top + tiny))).astype(bf16)
+                tops[d].append(top * held)
+    return tops
+
+
+def attend(place_ref, own_ref, col_ref, q0_ref, q1_ref, q2_ref, q3_ref, out_ref, kt_ref, v_ref, s_ref, p_ref, l_ref, h_ref):
     y, x, begin = place_ref[0], place_ref[1], place_ref[2]
     queries = (q0_ref, q1_ref, q2_ref, q3_ref)
     for j in range(NY):
@@ -181,9 +181,10 @@
                 stats = jnp.where(lane == (part * (CHUNK // PAGE) + g) * 3 + piece, rounded, stats)
                 one = one - rounded
         if part == per_set - 1:
-            out_ref[dest, ROWS:] = stats.astype(bf16)
+            out_ref[dest, ROWS : ROWS + PAGE] = stats.astype(bf16)
         return stats
 
+    tops = offer_pages(x, y, own_ref, col_ref, out_ref)
     stats = None
     for t in range(total + 2):
         if t >= 2:
@@ -194,10 +195,16 @@
             score(t)
         if 1 <= t < total + 1:
             weigh(t - 1)
+    narrow = lax.broadcasted_iota(jnp.int32, (TOK, HD), 1)
+    for d in range(NX):
+        rows = jnp.zeros((TOK, HD), f32)
+        for n, top in enumerate(tops[d]):
+            rows = jnp.where(narrow == n, top, rows)
+        out_ref[d, TOPS:] = rows.astype(bf16)
 
 
 def combine(in_ref, out_ref):
-    stats = [in_ref[i, ROWS:].astype(f32) for i in range(NX)]
+    stats = [in_ref[i, ROWS : ROWS + PAGE].astype(f32) for i in range(NX)]
     for g in range(GROUP):
         levels = [s[:, 3 * g : 3 * g + 1] + s[:, 3 * g + 1 : 3 * g + 2] + s[:, 3 * g + 2 : 3 * g + 3] for s in stats]
         top = jnp.maximum(jnp.maximum(levels[0], levels[1]), jnp.maximum(levels[2], levels[3]))
@@ -216,13 +223,19 @@
 
 def keep_pages(in_ref, store_ref, scale_ref):
     for slot in range(SLOTS):
-        store_ref[slot] = in_ref[slot * PAGE : (slot + 1) * PAGE]
+        for half in range(2):
+            at = ROWS + PAGE + (slot * 2 + half) * PAGE
+            part = in_ref[0, at : at + PAGE].astype(f32)
+            for i in range(1, NX):
+                part = part + in_ref[i, at : at + PAGE].astype(f32)
+            store_ref[slot, :, half * HD : (half + 1) * HD] = part.astype(bf16)
+    tops = in_ref[0, TOPS:].astype(f32)
+    for i in range(1, NX):
+        tops = tops + in_ref[i, TOPS:].astype(f32)
     row = lax.broadcasted_iota(jnp.int32, (2, 2), 0)
     col = lax.broadcasted_iota(jnp.int32, (2, 2), 1)
-    first = in_ref[SLOTS * PAGE : SLOTS * PAGE + TOK].astype(f32)
-    second = in_ref[SLOTS * PAGE + TOK :].astype(f32)
-    upper = jnp.where(col == 0, first[:1, :1], first[:1, HD : HD + 1])
-    lower = jnp.where(col == 0, second[:1, :1], second[:1, HD : HD + 1])
+    upper = jnp.where(col == 0, tops[:1, 0:1], tops[:1, 1:2])
+    lower = jnp.where(col == 0, tops[:1, 2:3], tops[:1, 3:4])
     scale_ref[...] = jnp.where(row == 0, upper, lower).astype(bf16)
 
 
@@ -231,17 +244,16 @@
     begin = offset[0]
     position = (begin + (y * NX + x) * PAGE + s * TOK).reshape(1)
     place = jnp.stack([y, x, begin]).astype(jnp.int32)
-    half = np.arange(HD // 2, dtype=np.float64) * 2.0 / HD
-    inverse = np.tile((rope_base ** (-half)).astype(np.float32), 2)[None]
 
     packed = pl.pallas_call(
         pack,
         out_shape=shaped((KVH, TOK, QW + WIDE)),
-        in_specs=[spec(SMEM), spec(), spec(), spec()],
+        in_specs=[spec(SMEM), spec(pltpu.HBM), spec(pltpu.HBM)],
         out_specs=spec(),
-        compiler_params=params(),
+        scratch_shapes=[VMEM((TOK, HQ * HD), bf16), VMEM((TOK, KVH * WIDE), bf16), pltpu.SemaphoreType.DMA((2,))],
+        compiler_params=params(60),
         name="pack",
-    )(position, jnp.asarray(inverse), queries[0], slab_kv[0])
+    )(position, queries[0], slab_kv[0])
     grouped = lax.all_to_all(packed, "seq", 0, 0, tiled=True)
 
     kv_send, q_own = pl.pallas_call(
@@ -255,22 +267,10 @@
     column = lax.all_to_all(kv_send, "y", 0, 0, tiled=True)
     asked = [q_own] + [lax.ppermute(q_own, "x", [(i, (i - k) % NX) for i in range(NX)]) for k in range(1, NX)]
 
-    offered = pl.pallas_call(
-        offer_pages,
-        out_shape=shaped((NX, SLOTS * (PAGE + TOK), WIDE)),
-        in_specs=[spec(SMEM), spec(SMEM), spec()],
-        out_specs=spec(),
-        compiler_params=params(),
-        name="offer_pages",
-    )(place, owners, column)
-    delivered = lax.psum_scatter(
-        offered.reshape(NX * SLOTS * (PAGE + TOK), WIDE), "x", scatter_dimension=0, tiled=True
-    )
-
     parts = pl.pallas_call(
         attend,
-        out_shape=shaped((NX, ROWS + PAGE, HD)),
-        in_specs=[spec(SMEM)] + [spec()] * 5,
+        out_shape=shaped((NX, TOPS + TOK, HD)),
+        in_specs=[spec(SMEM), spec(SMEM)] + [spec()] * 5,
         out_specs=spec(),
         scratch_shapes=[
             VMEM((HD, KEYS), bf16),
@@ -283,7 +283,7 @@
         compiler_params=params(),
         cost_estimate=cost(4 * NX * ROWS * KEYS * HD, 4 << 20, NX * ROWS * KEYS),
         name="attend",
-    )(place, column, *asked)
+    )(place, owners, column, *asked)
     parts = lax.all_to_all(parts, "x", 0, 0, tiled=True)
     result = pl.pallas_call(
         combine,
@@ -309,7 +309,7 @@
         out_specs=(spec(), spec()),
         compiler_params=params(),
         name="keep_pages",
-    )(delivered)
+    )(parts)
     return attention[None], stored[None, None], scales[None, None]
 
 

time: 114 us -> 105 us (0.921)
  blocking collectives: 23.4 us -> 45.8 us
  between operations: 14.7 us -> 1.35 us
  waiting for transfers between devices: 28.5 us -> 19.6 us
  starting transfers between devices: 26.7 us -> 21.8 us
  local copies, waits for them, and re-layouts: 3.35 us -> 0.72 us
  Pallas kernels: 15.8 us -> 14.5 us
    all_to_all x0 -> x1, blocking collectives: none -> 22.1 us  [on_device(): parts = lax.all_to_all(parts, 'x', 0, 0, tiled=True)]
    all_to_all x1 -> x0, waiting for transfers between devices: 9.41 us -> none  [on_device(): parts = lax.all_to_all(parts, 'x', 0, 0, tiled=True)]
    all_to_all x1, waiting for transfers between devices: 3.52 us -> 9.85 us  [on_device(): back = lax.all_to_all(result, 'seq', 0, 0, tiled=True)]
    reduce_scatter x1 -> x0, waiting for transfers between devices: 5.79 us -> none  [on_device(): lax.psum_scatter(offered.reshape(NX * SLOTS * (PAGE + TOK), WIDE), 'x', s...]
    all_to_all x1 -> x0, starting transfers between devices: 4.9 us -> none  [on_device(): parts = lax.all_to_all(parts, 'x', 0, 0, tiled=True)]
    pallas_call x2 -> x1, Pallas kernels: 11.8 us -> 8.67 us  [on_device(): pl.pallas_call(attend, out_shape=shaped((NX, TOPS + TOK, HD)), in_specs=[...]
    unnamed x12 -> x4, local copies, waits for them, and re-layouts: 3.35 us -> 0.72 us
    pallas_call x1, Pallas kernels: 0.19 us -> 1.89 us  [on_device(): pl.pallas_call(pack, out_shape=shaped((KVH, TOK, QW + WIDE)), in_specs=[s...]
  transfers between devices with their start and end apart: 7 -> 5, of which waited for: 7 -> 5; matrix products, arithmetic and copies ran while one was open for 0% -> 0% of each run, Pallas kernels for 4% -> 1%
where the time goes in v3:
time: 105 us; the launch traced here: 104 us
  blocking collectives  45.8 us (44%)
  starting transfers between devices  21.8 us (21%)
  waiting for transfers between devices  19.6 us (19%)
  Pallas kernels  14.5 us (14%)
  between operations  1.35 us (1%)
    all_to_all x1, blocking collectives, on_device(): grouped = lax.all_to_all(packed, 'seq', 0, 0, tiled=True)  23.6 us
    all_to_all x1, blocking collectives, on_device(): parts = lax.all_to_all(parts, 'x', 0, 0, tiled=True)  22.1 us
    all_to_all x1, waiting for transfers between devices, on_device(): back = lax.all_to_all(result, 'seq', 0, 0, tiled=True)  9.85 us
    ppermute x3, waiting for transfers between devices, on_device(): lax.ppermute(q_own, 'x', [(i, (i - k) % NX) for i in range(NX)])  9.04 us
    pallas_call x1, Pallas kernels, on_device(): pl.pallas_call(attend, out_shape=shaped((NX, TOPS + TOK, HD)), in_specs=[...  8.67 us
    ppermute x3, starting transfers between devices, on_device(): lax.ppermute(q_own, 'x', [(i, (i - k) % NX) for i in range(NX)])  8.62 us
    all_to_all x1, starting transfers between devices, on_device(): column = lax.all_to_all(kv_send, 'y', 0, 0, tiled=True)  7.1 us
    all_to_all x1, starting transfers between devices, on_device(): back = lax.all_to_all(result, 'seq', 0, 0, tiled=True)  6.11 us
  transfers between devices with their start and end apart: 5, of which 5 were waited for; matrix products, arithmetic and copies ran while one was open for 0% of the time, Pallas kernels for 1%

profile of v3, /device:TPU:6, one launch (start us, length us, event | category | flops | bytes accessed | tf_op | source)
XLA Modules:
  0.0 103.8 jit_solution(11653619339626484437)
XLA Ops:
  0.6 0.0 copy-start.1
  1.3 1.9 %pack.1 = bf16[8,16,1280]{2,1,0:T(8,128)(2,1)} custom-call(s32[1]{0:T(128)} %bitcast.3.pos_ref, bf16[16,8192]{1,0:T(8,128)(2,1)} %bitcast.10, bf16[16,2048]{1,0:T(8,128)(2,1)} %bitcast.12), custom_call_target="tpu_custom_call" | custom-call | tf_op jit(solution)/shard_map/pack/pallas_call | solution.py:248
  3.2 23.6 %all_to_all.20.in_ref = bf16[8,16,1280]{2,1,0:T(8,128)(2,1)S(1)} all-to-all(bf16[8,16,1280]{2,1,0:T(8,128)(2,1)} %pack.1), channel_id=1, replica_groups=mesh['seq'=8,'y'=8,'x'=4,'rep'=2] {'seq'}, dimensions={0} | all-to-all | bytes 655360 | tf_op jit(solution)/shard_map/all_to_all | solution.py:257
  26.8 0.0 copy-start
  26.8 0.7 copy-done
  27.5 0.9 spread.1
  28.5 7.1 %all-to-all-start.1 = ((bf16[8,160,256]{2,1,0:T(8,128)(2,1)}), bf16[8,160,256]{2,1,0:T(8,128)(2,1)S(1)}, u32[]{:S(2)}, u32[]{:S(2)}) async-start(bf16[8,160,256]{2,1,0:T(8,128)(2,1)} %get-tuple-element.7), calls=%async_computation.1 | async-start | bytes 1310720 | tf_op jit(solution)/shard_map/all_to_all | solution.py:267
  35.6 2.4 %collective-permute-start.2 = (bf16[1024,128]{1,0:T(8,128)(2,1)S(1)}, bf16[1024,128]{1,0:T(8,128)(2,1)S(1)}, u32[]{:S(2)}, u32[]{:S(2)}) collective-permute-start(bf16[1024,128]{1,0:T(8,128)(2,1)S(1)} %get-tuple-element.8.q0_ref), channel_id=1, source_target_pairs={{0,2},{2,4},{4,6},{6,0},{1,3},{3,5},{5,7},{7,1},{8,10},{10,12},{12... | collective-permute-start | bytes 786440 | tf_op jit(solution)/shard_map/ppermute | solution.py:268
  37.9 4.3 %collective-permute-start.1 = (bf16[1024,128]{1,0:T(8,128)(2,1)S(1)}, bf16[1024,128]{1,0:T(8,128)(2,1)S(1)}, u32[]{:S(2)}, u32[]{:S(2)}) collective-permute-start(bf16[1024,128]{1,0:T(8,128)(2,1)S(1)} %get-tuple-element.8.q0_ref), channel_id=1, source_target_pairs={{0,4},{2,6},{4,0},{6,2},{1,5},{3,7},{5,1},{7,3},{8,12},{10,14},{12... | collective-permute-start | bytes 786440 | tf_op jit(solution)/shard_map/ppermute | solution.py:268
  42.3 1.9 %collective-permute-start = (bf16[1024,128]{1,0:T(8,128)(2,1)S(1)}, bf16[1024,128]{1,0:T(8,128)(2,1)S(1)}, u32[]{:S(2)}, u32[]{:S(2)}) collective-permute-start(bf16[1024,128]{1,0:T(8,128)(2,1)S(1)} %get-tuple-element.8.q0_ref), channel_id=1, source_target_pairs={{0,6},{2,0},{4,2},{6,4},{1,7},{3,1},{5,3},{7,5},{8,14},{10,8},{12,... | collective-permute-start | bytes 786440 | tf_op jit(solution)/shard_map/ppermute | solution.py:268
  44.2 0.1 pad_add_fusion.place_ref
  44.3 1.8 %collective-permute-done.2.q3_ref = bf16[1024,128]{1,0:T(8,128)(2,1)S(1)} collective-permute-done((bf16[1024,128]{1,0:T(8,128)(2,1)S(1)}, bf16[1024,128]{1,0:T(8,128)(2,1)S(1)}, u32[]{:S(2)}, u32[]{:S(2)}) %collective-permute-start.2) | collective-permute-done | bytes 262176 | tf_op jit(solution)/shard_map/ppermute | solution.py:268
  46.1 4.2 %collective-permute-done.1.q2_ref = bf16[1024,128]{1,0:T(8,128)(2,1)S(1)} collective-permute-done((bf16[1024,128]{1,0:T(8,128)(2,1)S(1)}, bf16[1024,128]{1,0:T(8,128)(2,1)S(1)}, u32[]{:S(2)}, u32[]{:S(2)}) %collective-permute-start.1) | collective-permute-done | bytes 262176 | tf_op jit(solution)/shard_map/ppermute | solution.py:268
  50.3 3.0 %collective-permute-done.q1_ref = bf16[1024,128]{1,0:T(8,128)(2,1)S(1)} collective-permute-done((bf16[1024,128]{1,0:T(8,128)(2,1)S(1)}, bf16[1024,128]{1,0:T(8,128)(2,1)S(1)}, u32[]{:S(2)}, u32[]{:S(2)}) %collective-permute-start) | collective-permute-done | bytes 262176 | tf_op jit(solution)/shard_map/ppermute | solution.py:268
  53.3 0.7 all-to-all-done.1.col_ref
  54.0 0.0 copy-done.1
  54.0 8.7 %attend.1 = bf16[4,1680,128]{2,1,0:T(8,128)(2,1)S(1)} custom-call(s32[3]{0:T(128)S(1)} %pad_add_fusion.place_ref, s32[1,32]{1,0:T(1,128)S(1)} %copy-done.1, bf16[8,160,256]{2,1,0:T(8,128)(2,1)S(1)} %all-to-all-done.1.col_ref, bf16[1024,128]{1,0:T(8,128)(2,1)S(1)} %get-tuple-element.8.q0_ref, bf16[1024,128]{1,0:T(8,128)(2,1)S(1)} %collective-permute-done.q1_ref, ...), custom_call_target="tpu_custom_call" | custom-call | flops 2684354560 | bytes 4194304 | tf_op jit(solution)/shard_map/attend/pallas_call | solution.py:270
  62.7 22.1 %all_to_all.21.in_ref = bf16[4,1680,128]{2,1,0:T(8,128)(2,1)S(1)} all-to-all(bf16[4,1680,128]{2,1,0:T(8,128)(2,1)S(1)} %attend.1), channel_id=1, replica_groups=mesh['seq'=8,'y'=8,'x'=4,'rep'=2] {'x'}, dimensions={0} | all-to-all | bytes 3440640 | tf_op jit(solution)/shard_map/all_to_all | solution.py:287
  84.8 1.5 %combine.1 = bf16[8,16,1024]{2,1,0:T(8,128)(2,1)} custom-call(bf16[4,1680,128]{2,1,0:T(8,128)(2,1)S(1)} %all_to_all.21.in_ref), custom_call_target="tpu_custom_call" | custom-call | tf_op jit(solution)/shard_map/combine/pallas_call | solution.py:288
  86.4 6.1 %all-to-all-start.3 = ((bf16[8,16,1024]{2,1,0:T(8,128)(2,1)}), bf16[8,16,1024]{2,1,0:T(8,128)(2,1)S(1)}, u32[]{:S(2)}, u32[]{:S(2)}) async-start(bf16[8,16,1024]{2,1,0:T(8,128)(2,1)} %combine.1), calls=%async_computation.3 | async-start | bytes 524288 | tf_op jit(solution)/shard_map/all_to_all | solution.py:296
  92.5 0.7 keep_pages.1
  93.2 9.8 %all-to-all-done.3.in_ref = bf16[8,16,1024]{2,1,0:T(8,128)(2,1)S(1)} async-done(((bf16[8,16,1024]{2,1,0:T(8,128)(2,1)}), bf16[8,16,1024]{2,1,0:T(8,128)(2,1)S(1)}, u32[]{:S(2)}, u32[]{:S(2)}) %all-to-all-start.3) | async-done | bytes 262176 | tf_op jit(solution)/shard_map/all_to_all | solution.py:296
  103.1 0.7 unpack.1
Async XLA Ops:
  0.6 53.4 %copy-start.1 = (s32[1,32]{1,0:T(1,128)S(1)}, s32[1,32]{1,0:T(1,128)}, u32[]{:S(2)}) copy-start(s32[1,32]{1,0:T(1,128)} %own_ref.1) | copy-start | bytes 388
  26.8 0.7 copy-start
  28.5 25.6 %all-to-all-start.1 = ((bf16[8,160,256]{2,1,0:T(8,128)(2,1)}), bf16[8,160,256]{2,1,0:T(8,128)(2,1)S(1)}, u32[]{:S(2)}, u32[]{:S(2)}) async-start(bf16[8,160,256]{2,1,0:T(8,128)(2,1)} %get-tuple-element.7), calls=%async_computation.1 | async-start | bytes 1310720 | tf_op jit(solution)/shard_map/all_to_all | solution.py:267
  35.6 10.6 %collective-permute-start.2 = (bf16[1024,128]{1,0:T(8,128)(2,1)S(1)}, bf16[1024,128]{1,0:T(8,128)(2,1)S(1)}, u32[]{:S(2)}, u32[]{:S(2)}) collective-permute-start(bf16[1024,128]{1,0:T(8,128)(2,1)S(1)} %get-tuple-element.8.q0_ref), channel_id=1, source_target_pairs={{0,2},{2,4},{4,6},{6,0},{1,3},{3,5},{5,7},{7,1},{8,10},{10,12},{12... | collective-permute-start | bytes 786440 | tf_op jit(solution)/shard_map/ppermute | solution.py:268
  37.9 12.4 %collective-permute-start.1 = (bf16[1024,128]{1,0:T(8,128)(2,1)S(1)}, bf16[1024,128]{1,0:T(8,128)(2,1)S(1)}, u32[]{:S(2)}, u32[]{:S(2)}) collective-permute-start(bf16[1024,128]{1,0:T(8,128)(2,1)S(1)} %get-tuple-element.8.q0_ref), channel_id=1, source_target_pairs={{0,4},{2,6},{4,0},{6,2},{1,5},{3,7},{5,1},{7,3},{8,12},{10,14},{12... | collective-permute-start | bytes 786440 | tf_op jit(solution)/shard_map/ppermute | solution.py:268
  42.3 11.1 %collective-permute-start = (bf16[1024,128]{1,0:T(8,128)(2,1)S(1)}, bf16[1024,128]{1,0:T(8,128)(2,1)S(1)}, u32[]{:S(2)}, u32[]{:S(2)}) collective-permute-start(bf16[1024,128]{1,0:T(8,128)(2,1)S(1)} %get-tuple-element.8.q0_ref), channel_id=1, source_target_pairs={{0,6},{2,0},{4,2},{6,4},{1,7},{3,1},{5,3},{7,5},{8,14},{10,8},{12,... | collective-permute-start | bytes 786440 | tf_op jit(solution)/shard_map/ppermute | solution.py:268
  86.4 16.7 %all-to-all-start.3 = ((bf16[8,16,1024]{2,1,0:T(8,128)(2,1)}), bf16[8,16,1024]{2,1,0:T(8,128)(2,1)S(1)}, u32[]{:S(2)}, u32[]{:S(2)}) async-start(bf16[8,16,1024]{2,1,0:T(8,128)(2,1)} %combine.1), calls=%async_computation.3 | async-start | bytes 524288 | tf_op jit(solution)/shard_map/all_to_all | solution.py:296

commit v4 on v3

v4 whole, which is shorter than its diff:
```python
import math

import jax
import jax.numpy as jnp
import numpy as np
from jax import lax
from jax.experimental import pallas as pl
from jax.experimental.pallas import tpu as pltpu
from jax.sharding import Mesh, PartitionSpec as P

HQ = 64
KVH = 8
HD = 128
PAGE = 128
GROUP = HQ // KVH
TOK = 16
WIDE = 2 * HD
QW = GROUP * HD
ROWS = GROUP * PAGE
NX = 4
NY = 8
PRE = 32
SLAB = NY * PAGE
KEYS = SLAB + NY * PRE
SLOTS = 2
CHUNK = 512
MESSAGE = (GROUP + 1) * TOK

rope_base = 1000000.0
tiny = 1e-06
masked = -1e30
to_exp2 = HD ** (-0.5) * math.log2(math.e)

VMEM = pltpu.VMEM
SMEM = pltpu.SMEM
f32 = jnp.float32
bf16 = jnp.bfloat16


def spec(space=VMEM):
    return pl.BlockSpec(memory_space=space)


def params(mib=32):
    return pltpu.CompilerParams(vmem_limit_bytes=mib * 1024 * 1024)


def cost(flops, moved, exps=0):
    return pl.CostEstimate(flops=flops, bytes_accessed=moved, transcendentals=exps)


def shaped(shape, dtype=bf16):
    return jax.ShapeDtypeStruct(shape, dtype)


def pack(offset_ref, q_hbm, kv_hbm, out_ref, q_ref, kv_ref, sems):
    block = lax.axis_index("y") * NX + lax.axis_index("x")
    first = offset_ref[0] + block * PAGE + lax.axis_index("seq") * TOK
    fetch_q = pltpu.make_async_copy(q_hbm, q_ref, sems.at[0])
    fetch_kv = pltpu.make_async_copy(kv_hbm, kv_ref, sems.at[1])
    fetch_q.start()
    fetch_kv.start()
    half = HD // 2
    lane = lax.broadcasted_iota(jnp.int32, (TOK, HD), 1)
    place = lane % half
    inverse = jnp.zeros((TOK, HD), f32)
    for k in range(half):
        inverse = jnp.where(place == k, float(np.float32(rope_base ** (-2.0 * k / HD))), inverse)
    row = lax.broadcasted_iota(jnp.int32, (TOK, HD), 0) + first
    angles = row.astype(f32) * inverse
    cosine = jnp.cos(angles)
    sinus = jnp.sin(angles)
    sinus = jnp.where(lane < half, -sinus, sinus)

    def turn(x):
        x = x.astype(f32)
        return (x * cosine + pltpu.roll(x, half, 1) * sinus).astype(bf16)

    fetch_kv.wait()
    for h in range(KVH):
        out_ref[h, :, QW : QW + HD] = turn(kv_ref[:, h * WIDE : h * WIDE + HD])
        out_ref[h, :, QW + HD :] = kv_ref[:, h * WIDE + HD : (h + 1) * WIDE]
    fetch_q.wait()
    for h in range(KVH):
        for g in range(GROUP):
            q = h * GROUP + g
            out_ref[h, :, g * HD : (g + 1) * HD] = turn(q_ref[:, q * HD : (q + 1) * HD])


def spread(in_ref, pre_ref, kv_ref, q_ref):
    own = in_ref[:, :, QW:].reshape(PAGE, WIDE)
    pre = pre_ref[...]
    for j in range(NY):
        kv_ref[j, :PAGE] = own
        kv_ref[j, PAGE:] = pre
    for g in range(GROUP):
        q_ref[g * PAGE : (g + 1) * PAGE] = in_ref[:, :, g * HD : (g + 1) * HD].reshape(PAGE, HD)


def offer_pages(place_ref, own_ref, col_ref, *outs):
    y, x = place_ref[0], place_ref[1]
    pages = own_ref.shape[1]
    found = [[jnp.int32(pages)] * SLOTS for _ in range(NX)]
    owners = [y * NX + (x + k) % NX for k in range(NX)]
    for p in reversed(range(pages)):
        for k in range(NX):
            hit = own_ref[0, p] == owners[k]
            one, two = found[k]
            found[k] = [jnp.where(hit, p, one), jnp.where(hit, one, two)]
    lane = lax.broadcasted_iota(jnp.int32, (TOK, WIDE), 1)
    for k in range(NX):
        tops = jnp.zeros((TOK, WIDE), f32)
        for slot in range(SLOTS):
            page = found[k][slot]
            held = jnp.where((page < pages) & (page % NX == x), 1.0, 0.0)
            row = jnp.minimum(page // NX, NY - 1)
            for half in range(2):
                part = col_ref[row, :PAGE, half * HD : (half + 1) * HD].astype(f32)
                top = jnp.max(jnp.max(jnp.abs(part), axis=0, keepdims=True), axis=1, keepdims=True)
                scaled = part * (held / (top + tiny))
                outs[k][slot * PAGE : (slot + 1) * PAGE, half * HD : (half + 1) * HD] = scaled.astype(bf16)
                tops = jnp.where(lane == slot * 2 + half, top * held, tops)
        outs[k][SLOTS * PAGE :] = tops.astype(bf16)


def attend(place_ref, col_ref, *refs):
    *queries, out_ref, kt_ref, v_ref, s_ref, p_ref, l_ref, h_ref = refs
    y, x, begin = place_ref[0], place_ref[1], place_ref[2]
    for j in range(NY):
        b = (y + j) % NY
        kt_ref[:, j * PAGE : (j + 1) * PAGE] = col_ref[b, :PAGE, :HD].T
        v_ref[j * PAGE : (j + 1) * PAGE] = col_ref[b, :PAGE, HD:]
    kt_ref[:, SLAB:] = col_ref[:, PAGE:, :HD].reshape(NY * PRE, HD).T
    v_ref[SLAB:] = col_ref[:, PAGE:, HD:].reshape(NY * PRE, HD)

    c = lax.broadcasted_iota(jnp.int32, (1, KEYS), 1)
    b = (y + c // PAGE) % NY
    i = c - SLAB
    slab_bias = jnp.where(c < PAGE, 0.0, jnp.where(b < y, 0.0, masked))
    prefix_bias = jnp.where(((i // PRE) * NX + x) * PRE + i % PRE < begin, 0.0, masked)
    bias = jnp.where(c < SLAB, slab_bias, prefix_bias)
    token = lax.broadcasted_iota(jnp.int32, (CHUNK, PAGE), 0) % PAGE
    own_key = lax.broadcasted_iota(jnp.int32, (CHUNK, PAGE), 1)
    lane = lax.broadcasted_iota(jnp.int32, (PAGE, HD), 1)
    per_set = ROWS // CHUNK
    total = NX * per_set

    def score(t):
        n, part = divmod(t, per_set)
        q = queries[n][part * CHUNK : (part + 1) * CHUNK]
        s = jnp.dot(q, kt_ref[...], preferred_element_type=f32) + bias
        at = slice(t % 2 * CHUNK, (t % 2 + 1) * CHUNK)
        if n == 0:
            s_ref[at, :PAGE] = jnp.where(own_key <= token, s[:, :PAGE], masked)
        else:
            s_ref[at, :PAGE] = s[:, :PAGE] + jnp.where((x + n) % NX > x, 0.0, masked)
        s_ref[at, PAGE:] = s[:, PAGE:]

    def weigh(t):
        at = slice(t % 2 * CHUNK, (t % 2 + 1) * CHUNK)
        s = s_ref[at, :]
        top = s[:, :HD]
        for n in range(1, KEYS // HD):
            top = jnp.maximum(top, s[:, n * HD : (n + 1) * HD])
        high = jnp.max(top, axis=1, keepdims=True) * to_exp2
        p = jnp.exp2(s * to_exp2 - high)
        mass = p[:, :HD]
        for n in range(1, KEYS // HD):
            mass = mass + p[:, n * HD : (n + 1) * HD]
        l_ref[at, :] = mass
        h_ref[at, :] = jnp.broadcast_to(high, (CHUNK, HD))
        p_ref[at, :] = p.astype(bf16)

    def gather(t, stats):
        n, part = divmod(t, per_set)

        def put(g, value):
            out_ref[:, (x + n) % NX, g * TOK : (g + 1) * TOK] = value.reshape(KVH, TOK, HD)

        at = slice(t % 2 * CHUNK, (t % 2 + 1) * CHUNK)
        num = jnp.dot(p_ref[at, :], v_ref[...], preferred_element_type=f32)
        mass = jnp.sum(l_ref[at, :], axis=1, keepdims=True)
        done = (num / mass).astype(bf16)
        level = h_ref[at, :] + jnp.log2(mass)
        for m in range(CHUNK // PAGE):
            g = part * (CHUNK // PAGE) + m
            rows = slice(m * PAGE, (m + 1) * PAGE)
            put(g, done[rows])
            one = level[rows]
            for piece in range(3):
                rounded = one.astype(bf16).astype(f32)
                stats = jnp.where(lane == piece * GROUP + g, rounded, stats)
                one = one - rounded
        if part == per_set - 1:
            put(GROUP, stats.astype(bf16))
        return stats

    stats = None
    for t in range(total + 2):
        if t >= 2:
            if (t - 2) % per_set == 0:
                stats = jnp.zeros((PAGE, HD), f32)
            stats = gather(t - 2, stats)
        if t < total:
            score(t)
        if 1 <= t < total + 1:
            weigh(t - 1)


def combine(in_ref, out_ref):
    for h in range(KVH):
        levels = []
        for i in range(NX):
            pieces = in_ref[h * NX + i, GROUP * TOK :].astype(f32)
            levels.append(pieces + pltpu.roll(pieces, HD - GROUP, 1) + pltpu.roll(pieces, HD - 2 * GROUP, 1))
        top = jnp.maximum(jnp.maximum(levels[0], levels[1]), jnp.maximum(levels[2], levels[3]))
        shares = [jnp.exp2(v - top) for v in levels]
        whole = shares[0] + shares[1] + shares[2] + shares[3]
        shares = [v / whole for v in shares]
        for g in range(GROUP):
            done = jnp.zeros((TOK, HD), f32)
            for i in range(NX):
                part = in_ref[h * NX + i, g * TOK : (g + 1) * TOK].astype(f32)
                done = done + part * shares[i][:, g : g + 1]
            out_ref[:, h * QW + g * HD : h * QW + (g + 1) * HD] = done.astype(bf16)


def keep_pages(*refs):
    *ins, store_ref, scale_ref = refs

    def total(at):
        part = ins[0][at].astype(f32)
        for ref in ins[1:]:
            part = part + ref[at].astype(f32)
        return part

    for slot in range(SLOTS):
        store_ref[slot] = total(slice(slot * PAGE, (slot + 1) * PAGE)).astype(bf16)
    tops = total(slice(SLOTS * PAGE, SLOTS * PAGE + TOK))
    row = lax.broadcasted_iota(jnp.int32, (2, 2), 0)
    col = lax.broadcasted_iota(jnp.int32, (2, 2), 1)
    upper = jnp.where(col == 0, tops[:1, 0:1], tops[:1, 1:2])
    lower = jnp.where(col == 0, tops[:1, 2:3], tops[:1, 3:4])
    scale_ref[...] = jnp.where(row == 0, upper, lower).astype(bf16)


def on_device(queries, slab_kv, prefix_kv, owners, offset):
    y, x = lax.axis_index("y"), lax.axis_index("x")
    begin = offset[0]
    place = jnp.stack([y, x, begin]).astype(jnp.int32)

    packed = pl.pallas_call(
        pack,
        out_shape=shaped((KVH, TOK, QW + WIDE)),
        in_specs=[spec(SMEM), spec(pltpu.HBM), spec(pltpu.HBM)],
        out_specs=spec(),
        scratch_shapes=[VMEM((TOK, HQ * HD), bf16), VMEM((TOK, KVH * WIDE), bf16), pltpu.SemaphoreType.DMA((2,))],
        compiler_params=params(60),
        name="pack",
    )(offset, queries[0], slab_kv[0])
    grouped = lax.all_to_all(packed, "seq", 0, 0, tiled=True)

    kv_send, q_own = pl.pallas_call(
        spread,
        out_shape=(shaped((NY, PAGE + PRE, WIDE)), shaped((ROWS, HD))),
        in_specs=[spec(), spec()],
        out_specs=(spec(), spec()),
        compiler_params=params(),
        name="spread",
    )(grouped, prefix_kv)
    column = lax.all_to_all(kv_send, "y", 0, 0, tiled=True)
    asked = [q_own] + [lax.ppermute(q_own, "x", [(i, (i - k) % NX) for i in range(NX)]) for k in range(1, NX)]

    parts = pl.pallas_call(
        attend,
        out_shape=shaped((KVH, NX, MESSAGE, HD)),
        in_specs=[spec(SMEM)] + [spec()] * (1 + NX),
        out_specs=spec(),
        scratch_shapes=[
            VMEM((HD, KEYS), bf16),
            VMEM((KEYS, HD), bf16),
            VMEM((2 * CHUNK, KEYS), f32),
            VMEM((2 * CHUNK, KEYS), bf16),
            VMEM((2 * CHUNK, HD), f32),
            VMEM((2 * CHUNK, HD), f32),
        ],
        compiler_params=params(),
        cost_estimate=cost(4 * NX * ROWS * KEYS * HD, 4 << 20, NX * ROWS * KEYS),
        name="attend",
    )(place, column, *asked)
    parts = lax.all_to_all(parts.reshape(KVH * NX, MESSAGE, HD), ("seq", "x"), 0, 0, tiled=True)

    offered = pl.pallas_call(
        offer_pages,
        out_shape=(shaped((SLOTS * PAGE + TOK, WIDE)),) * NX,
        in_specs=[spec(SMEM), spec(SMEM), spec()],
        out_specs=(spec(),) * NX,
        compiler_params=params(),
        name="offer_pages",
    )(place, owners, column)
    delivered = [offered[0]] + [
        lax.ppermute(offered[k], "x", [(i, (i + k) % NX) for i in range(NX)]) for k in range(1, NX)
    ]
    stored, scales = pl.pallas_call(
        keep_pages,
        out_shape=(shaped((SLOTS, PAGE, WIDE)), shaped((2, 2))),
        in_specs=[spec()] * NX,
        out_specs=(spec(), spec()),
        compiler_params=params(),
        name="keep_pages",
    )(*delivered)
    attention = pl.pallas_call(
        combine,
        out_shape=shaped((TOK, HQ * HD)),
        in_specs=[spec()],
        out_specs=spec(),
        compiler_params=params(),
        name="combine",
    )(parts)
    return attention[None], stored[None, None], scales[None, None]


def solution(mesh):
    sizes = mesh.shape
    devices = mesh.devices.reshape(sizes["seq"], NY, NX, sizes["rep"])
    whole = Mesh(devices, ("seq", "y", "x", "rep"))
    dec = ("y", "x")
    return jax.shard_map(
        on_device,
        mesh=whole,
        in_specs=(
            P(("rep",) + dec, "seq", None),
            P(("rep",) + dec, "seq", None),
            P(("rep",) + dec, "seq"),
            P(("rep", "seq"), None),
            P("rep"),
        ),
        out_specs=(
            P(("rep",) + dec, "seq", None),
            P(("rep", "seq"), dec, None, None, None),
            P(("rep", "seq"), dec, None, None),
        ),
        check_vma=False,
    )
```

time: 105 us -> 103 us (0.981)
  blocking collectives: 45.8 us -> 23.6 us
  waiting for transfers between devices: 19.6 us -> 30.4 us
  starting transfers between devices: 21.8 us -> 30.9 us
  Pallas kernels: 14.5 us -> 16.3 us
    all_to_all x1 -> x0, blocking collectives: 22.1 us -> none  [on_device(): parts = lax.all_to_all(parts, 'x', 0, 0, tiled=True)]
    ppermute x0 -> x3, waiting for transfers between devices: none -> 10.6 us  [on_device(): lax.ppermute(offered[k], 'x', [(i, (i + k) % NX) for i in range(NX)])]
    ppermute x0 -> x3, starting transfers between devices: none -> 8.66 us  [on_device(): lax.ppermute(offered[k], 'x', [(i, (i + k) % NX) for i in range(NX)])]
    pallas_call x3, Pallas kernels: 10.9 us -> 12.7 us  [the longest x1 9.3 us: on_device(): pl.pallas_call(attend, out_shape=shaped((KVH, NX, MESSAGE, HD)), in_specs...]
  transfers between devices with their start and end apart: 5 -> 8, of which waited for: 5 -> 8; matrix products, arithmetic and copies ran while one was open for 0% -> 0% of each run, Pallas kernels for 1% -> 2%
where the time goes in v4:
time: 103 us
  starting transfers between devices  30.9 us (30%)
  waiting for transfers between devices  30.4 us (30%)
  blocking collectives  23.6 us (23%)
  Pallas kernels  16.3 us (16%)
  between operations  1.39 us (1%)
    all_to_all x1, blocking collectives, on_device(): grouped = lax.all_to_all(packed, 'seq', 0, 0, tiled=True)  23.6 us
    ppermute x3, waiting for transfers between devices, on_device(): lax.ppermute(offered[k], 'x', [(i, (i + k) % NX) for i in range(NX)])  10.6 us
    all_to_all x1, waiting for transfers between devices, on_device(): lax.all_to_all(parts.reshape(KVH * NX, MESSAGE, HD), ('seq', 'x'), 0, 0,...  10.1 us
    pallas_call x1, Pallas kernels, on_device(): pl.pallas_call(attend, out_shape=shaped((KVH, NX, MESSAGE, HD)), in_specs...  9.3 us
    ppermute x3, waiting for transfers between devices, on_device(): lax.ppermute(q_own, 'x', [(i, (i - k) % NX) for i in range(NX)])  9.04 us
    ppermute x3, starting transfers between devices, on_device(): lax.ppermute(offered[k], 'x', [(i, (i + k) % NX) for i in range(NX)])  8.66 us
    ppermute x3, starting transfers between devices, on_device(): lax.ppermute(q_own, 'x', [(i, (i - k) % NX) for i in range(NX)])  8.62 us
    all_to_all x1, starting transfers between devices, on_device(): column = lax.all_to_all(kv_send, 'y', 0, 0, tiled=True)  7.1 us
  transfers between devices with their start and end apart: 8, of which 8 were waited for; matrix products, arithmetic and copies ran while one was open for 0% of the time, Pallas kernels for 2%

profile of v4, /device:TPU:6, one launch (start us, length us, event | category | flops | bytes accessed | tf_op | source)
XLA Modules:
  0.0 102.7 jit_solution(17290906790148138333)
XLA Ops:
  0.6 0.0 copy-start
  1.3 1.9 %pack.1 = bf16[8,16,1280]{2,1,0:T(8,128)(2,1)} custom-call(s32[1]{0:T(128)S(6)} %copy.8.offset_ref, bf16[16,8192]{1,0:T(8,128)(2,1)} %bitcast.8, bf16[16,2048]{1,0:T(8,128)(2,1)} %bitcast.10), custom_call_target="tpu_custom_call" | custom-call | tf_op jit(solution)/shard_map/pack/pallas_call | solution.py:252
  3.2 23.6 %all_to_all.15.in_ref = bf16[8,16,1280]{2,1,0:T(8,128)(2,1)S(1)} all-to-all(bf16[8,16,1280]{2,1,0:T(8,128)(2,1)} %pack.1), channel_id=1, replica_groups=mesh['seq'=8,'y'=8,'x'=4,'rep'=2] {'seq'}, dimensions={0} | all-to-all | bytes 655360 | tf_op jit(solution)/shard_map/all_to_all | solution.py:261
  26.8 0.0 copy-done
  26.8 0.9 spread.1
  27.7 7.1 %all-to-all-start.1 = ((bf16[8,160,256]{2,1,0:T(8,128)(2,1)}), bf16[8,160,256]{2,1,0:T(8,128)(2,1)S(1)}, u32[]{:S(2)}, u32[]{:S(2)}) async-start(bf16[8,160,256]{2,1,0:T(8,128)(2,1)} %get-tuple-element.11), calls=%async_computation.1 | async-start | bytes 1310720 | tf_op jit(solution)/shard_map/all_to_all | solution.py:271
  34.8 2.4 %collective-permute-start.2 = (bf16[1024,128]{1,0:T(8,128)(2,1)S(1)}, bf16[1024,128]{1,0:T(8,128)(2,1)S(1)}, u32[]{:S(2)}, u32[]{:S(2)}) collective-permute-start(bf16[1024,128]{1,0:T(8,128)(2,1)S(1)} %get-tuple-element.12.refs_0_), channel_id=1, source_target_pairs={{0,2},{2,4},{4,6},{6,0},{1,3},{3,5},{5,7},{7,1},{8,10},{10,12},{12... | collective-permute-start | bytes 786440 | tf_op jit(solution)/shard_map/ppermute | solution.py:272
  37.2 4.3 %collective-permute-start.1 = (bf16[1024,128]{1,0:T(8,128)(2,1)S(1)}, bf16[1024,128]{1,0:T(8,128)(2,1)S(1)}, u32[]{:S(2)}, u32[]{:S(2)}) collective-permute-start(bf16[1024,128]{1,0:T(8,128)(2,1)S(1)} %get-tuple-element.12.refs_0_), channel_id=1, source_target_pairs={{0,4},{2,6},{4,0},{6,2},{1,5},{3,7},{5,1},{7,3},{8,12},{10,14},{12... | collective-permute-start | bytes 786440 | tf_op jit(solution)/shard_map/ppermute | solution.py:272
  41.5 1.9 %collective-permute-start = (bf16[1024,128]{1,0:T(8,128)(2,1)S(1)}, bf16[1024,128]{1,0:T(8,128)(2,1)S(1)}, u32[]{:S(2)}, u32[]{:S(2)}) collective-permute-start(bf16[1024,128]{1,0:T(8,128)(2,1)S(1)} %get-tuple-element.12.refs_0_), channel_id=1, source_target_pairs={{0,6},{2,0},{4,2},{6,4},{1,7},{3,1},{5,3},{7,5},{8,14},{10,8},{12,... | collective-permute-start | bytes 786440 | tf_op jit(solution)/shard_map/ppermute | solution.py:272
  43.5 0.1 pad_add_fusion.place_ref
  43.6 1.8 %collective-permute-done.2.refs_3_ = bf16[1024,128]{1,0:T(8,128)(2,1)S(1)} collective-permute-done((bf16[1024,128]{1,0:T(8,128)(2,1)S(1)}, bf16[1024,128]{1,0:T(8,128)(2,1)S(1)}, u32[]{:S(2)}, u32[]{:S(2)}) %collective-permute-start.2) | collective-permute-done | bytes 262176 | tf_op jit(solution)/shard_map/ppermute | solution.py:272
  45.4 4.2 %collective-permute-done.1.refs_2_ = bf16[1024,128]{1,0:T(8,128)(2,1)S(1)} collective-permute-done((bf16[1024,128]{1,0:T(8,128)(2,1)S(1)}, bf16[1024,128]{1,0:T(8,128)(2,1)S(1)}, u32[]{:S(2)}, u32[]{:S(2)}) %collective-permute-start.1) | collective-permute-done | bytes 262176 | tf_op jit(solution)/shard_map/ppermute | solution.py:272
  49.6 3.0 %collective-permute-done.refs_1_ = bf16[1024,128]{1,0:T(8,128)(2,1)S(1)} collective-permute-done((bf16[1024,128]{1,0:T(8,128)(2,1)S(1)}, bf16[1024,128]{1,0:T(8,128)(2,1)S(1)}, u32[]{:S(2)}, u32[]{:S(2)}) %collective-permute-start) | collective-permute-done | bytes 262176 | tf_op jit(solution)/shard_map/ppermute | solution.py:272
  52.6 0.7 all-to-all-done.1.col_ref
  53.3 9.3 %attend.1 = bf16[8,4,144,128]{3,2,1,0:T(8,128)(2,1)} custom-call(s32[3]{0:T(128)S(1)} %pad_add_fusion.place_ref, bf16[8,160,256]{2,1,0:T(8,128)(2,1)S(1)} %all-to-all-done.1.col_ref, bf16[1024,128]{1,0:T(8,128)(2,1)S(1)} %get-tuple-element.12.refs_0_, bf16[1024,128]{1,0:T(8,128)(2,1)S(1)} %collective-permute-done.refs_1_, ...), custom_call_target="tpu_custom_call" | custom-call | flops 2684354560 | bytes 4194304 | tf_op jit(solution)/shard_map/attend/pallas_call | solution.py:274
  62.6 0.0 copy-start.1
  62.6 6.5 %all-to-all-start.2 = ((bf16[32,144,128]{2,1,0:T(8,128)(2,1)}), bf16[32,144,128]{2,1,0:T(8,128)(2,1)S(1)}, u32[]{:S(2)}, u32[]{:S(2)}) async-start(bf16[32,144,128]{2,1,0:T(8,128)(2,1)} %bitcast.4), calls=%async_computation.2 | async-start | bytes 2359296 | tf_op jit(solution)/shard_map/all_to_all | solution.py:291
  69.1 0.0 copy-done.1
  69.1 0.9 offer_pages.1
  70.0 2.1 %collective-permute-start.3 = (bf16[272,256]{1,0:T(8,128)(2,1)S(1)}, bf16[272,256]{1,0:T(8,128)(2,1)S(1)}, u32[]{:S(2)}, u32[]{:S(2)}) collective-permute-start(bf16[272,256]{1,0:T(8,128)(2,1)S(1)} %get-tuple-element.14), channel_id=1, source_target_pairs={{0,2},{2,4},{4,6},{6,0},{1,3},{3,5},{5,7},{7,1},{8,10},{10,12},{12... | collective-permute-start | bytes 417800 | tf_op jit(solution)/shard_map/ppermute | solution.py:302
  72.2 4.6 %collective-permute-start.4 = (bf16[272,256]{1,0:T(8,128)(2,1)S(1)}, bf16[272,256]{1,0:T(8,128)(2,1)S(1)}, u32[]{:S(2)}, u32[]{:S(2)}) collective-permute-start(bf16[272,256]{1,0:T(8,128)(2,1)S(1)} %get-tuple-element.15), channel_id=1, source_target_pairs={{0,4},{2,6},{4,0},{6,2},{1,5},{3,7},{5,1},{7,3},{8,12},{10,14},{12... | collective-permute-start | bytes 417800 | tf_op jit(solution)/shard_map/ppermute | solution.py:302
  76.8 1.9 %collective-permute-start.5 = (bf16[272,256]{1,0:T(8,128)(2,1)S(1)}, bf16[272,256]{1,0:T(8,128)(2,1)S(1)}, u32[]{:S(2)}, u32[]{:S(2)}) collective-permute-start(bf16[272,256]{1,0:T(8,128)(2,1)S(1)} %get-tuple-element.16), channel_id=1, source_target_pairs={{0,6},{2,0},{4,2},{6,4},{1,7},{3,1},{5,3},{7,5},{8,14},{10,8},{12,... | collective-permute-start | bytes 417800 | tf_op jit(solution)/shard_map/ppermute | solution.py:302
  78.7 2.3 %collective-permute-done.3.refs_1_ = bf16[272,256]{1,0:T(8,128)(2,1)S(1)} collective-permute-done((bf16[272,256]{1,0:T(8,128)(2,1)S(1)}, bf16[272,256]{1,0:T(8,128)(2,1)S(1)}, u32[]{:S(2)}, u32[]{:S(2)}) %collective-permute-start.3) | collective-permute-done | bytes 139296 | tf_op jit(solution)/shard_map/ppermute | solution.py:302
  81.0 3.1 %collective-permute-done.4.refs_2_ = bf16[272,256]{1,0:T(8,128)(2,1)S(1)} collective-permute-done((bf16[272,256]{1,0:T(8,128)(2,1)S(1)}, bf16[272,256]{1,0:T(8,128)(2,1)S(1)}, u32[]{:S(2)}, u32[]{:S(2)}) %collective-permute-start.4) | collective-permute-done | bytes 139296 | tf_op jit(solution)/shard_map/ppermute | solution.py:302
  84.1 5.2 %collective-permute-done.5.refs_3_ = bf16[272,256]{1,0:T(8,128)(2,1)S(1)} collective-permute-done((bf16[272,256]{1,0:T(8,128)(2,1)S(1)}, bf16[272,256]{1,0:T(8,128)(2,1)S(1)}, u32[]{:S(2)}, u32[]{:S(2)}) %collective-permute-start.5) | collective-permute-done | bytes 139296 | tf_op jit(solution)/shard_map/ppermute | solution.py:302
  89.3 0.8 keep_pages.1
  90.1 10.1 %all-to-all-done.2.in_ref = bf16[32,144,128]{2,1,0:T(8,128)(2,1)S(1)} async-done(((bf16[32,144,128]{2,1,0:T(8,128)(2,1)}), bf16[32,144,128]{2,1,0:T(8,128)(2,1)S(1)}, u32[]{:S(2)}, u32[]{:S(2)}) %all-to-all-start.2) | async-done | bytes 1179680 | tf_op jit(solution)/shard_map/all_to_all | solution.py:291
  100.2 2.5 %combine.1 = bf16[16,8192]{1,0:T(8,128)(2,1)} custom-call(bf16[32,144,128]{2,1,0:T(8,128)(2,1)S(1)} %all-to-all-done.2.in_ref), custom_call_target="tpu_custom_call" | custom-call | tf_op jit(solution)/shard_map/combine/pallas_call | solution.py:312
Async XLA Ops:
  0.6 26.2 %copy-start = (bf16[32,256]{1,0:T(8,128)(2,1)S(1)}, bf16[32,256]{1,0:T(8,128)(2,1)}, u32[]{:S(2)}) copy-start(bf16[32,256]{1,0:T(8,128)(2,1)} %pre_ref.1) | copy-start | bytes 49156
  27.7 25.6 %all-to-all-start.1 = ((bf16[8,160,256]{2,1,0:T(8,128)(2,1)}), bf16[8,160,256]{2,1,0:T(8,128)(2,1)S(1)}, u32[]{:S(2)}, u32[]{:S(2)}) async-start(bf16[8,160,256]{2,1,0:T(8,128)(2,1)} %get-tuple-element.11), calls=%async_computation.1 | async-start | bytes 1310720 | tf_op jit(solution)/shard_map/all_to_all | solution.py:271
  34.8 10.6 %collective-permute-start.2 = (bf16[1024,128]{1,0:T(8,128)(2,1)S(1)}, bf16[1024,128]{1,0:T(8,128)(2,1)S(1)}, u32[]{:S(2)}, u32[]{:S(2)}) collective-permute-start(bf16[1024,128]{1,0:T(8,128)(2,1)S(1)} %get-tuple-element.12.refs_0_), channel_id=1, source_target_pairs={{0,2},{2,4},{4,6},{6,0},{1,3},{3,5},{5,7},{7,1},{8,10},{10,12},{12... | collective-permute-start | bytes 786440 | tf_op jit(solution)/shard_map/ppermute | solution.py:272
  37.2 12.4 %collective-permute-start.1 = (bf16[1024,128]{1,0:T(8,128)(2,1)S(1)}, bf16[1024,128]{1,0:T(8,128)(2,1)S(1)}, u32[]{:S(2)}, u32[]{:S(2)}) collective-permute-start(bf16[1024,128]{1,0:T(8,128)(2,1)S(1)} %get-tuple-element.12.refs_0_), channel_id=1, source_target_pairs={{0,4},{2,6},{4,0},{6,2},{1,5},{3,7},{5,1},{7,3},{8,12},{10,14},{12... | collective-permute-start | bytes 786440 | tf_op jit(solution)/shard_map/ppermute | solution.py:272
  41.5 11.1 %collective-permute-start = (bf16[1024,128]{1,0:T(8,128)(2,1)S(1)}, bf16[1024,128]{1,0:T(8,128)(2,1)S(1)}, u32[]{:S(2)}, u32[]{:S(2)}) collective-permute-start(bf16[1024,128]{1,0:T(8,128)(2,1)S(1)} %get-tuple-element.12.refs_0_), channel_id=1, source_target_pairs={{0,6},{2,0},{4,2},{6,4},{1,7},{3,1},{5,3},{7,5},{8,14},{10,8},{12,... | collective-permute-start | bytes 786440 | tf_op jit(solution)/shard_map/ppermute | solution.py:272
  62.6 6.5 %copy-start.1 = (s32[1,32]{1,0:T(1,128)S(1)}, s32[1,32]{1,0:T(1,128)}, u32[]{:S(2)}) copy-start(s32[1,32]{1,0:T(1,128)} %own_ref.1) | copy-start | bytes 388
  62.6 37.6 %all-to-all-start.2 = ((bf16[32,144,128]{2,1,0:T(8,128)(2,1)}), bf16[32,144,128]{2,1,0:T(8,128)(2,1)S(1)}, u32[]{:S(2)}, u32[]{:S(2)}) async-start(bf16[32,144,128]{2,1,0:T(8,128)(2,1)} %bitcast.4), calls=%async_computation.2 | async-start | bytes 2359296 | tf_op jit(solution)/shard_map/all_to_all | solution.py:291
  70.0 11.0 %collective-permute-start.3 = (bf16[272,256]{1,0:T(8,128)(2,1)S(1)}, bf16[272,256]{1,0:T(8,128)(2,1)S(1)}, u32[]{:S(2)}, u32[]{:S(2)}) collective-permute-start(bf16[272,256]{1,0:T(8,128)(2,1)S(1)} %get-tuple-element.14), channel_id=1, source_target_pairs={{0,2},{2,4},{4,6},{6,0},{1,3},{3,5},{5,7},{7,1},{8,10},{10,12},{12... | collective-permute-start | bytes 417800 | tf_op jit(solution)/shard_map/ppermute | solution.py:302
  72.2 11.9 %collective-permute-start.4 = (bf16[272,256]{1,0:T(8,128)(2,1)S(1)}, bf16[272,256]{1,0:T(8,128)(2,1)S(1)}, u32[]{:S(2)}, u32[]{:S(2)}) collective-permute-start(bf16[272,256]{1,0:T(8,128)(2,1)S(1)} %get-tuple-element.15), channel_id=1, source_target_pairs={{0,4},{2,6},{4,0},{6,2},{1,5},{3,7},{5,1},{7,3},{8,12},{10,14},{12... | collective-permute-start | bytes 417800 | tf_op jit(solution)/shard_map/ppermute | solution.py:302
  76.8 12.5 %collective-permute-start.5 = (bf16[272,256]{1,0:T(8,128)(2,1)S(1)}, bf16[272,256]{1,0:T(8,128)(2,1)S(1)}, u32[]{:S(2)}, u32[]{:S(2)}) collective-permute-start(bf16[272,256]{1,0:T(8,128)(2,1)S(1)} %get-tuple-element.16), channel_id=1, source_target_pairs={{0,6},{2,0},{4,2},{6,4},{1,7},{3,1},{5,3},{7,5},{8,14},{10,8},{12,... | collective-permute-start | bytes 417800 | tf_op jit(solution)/shard_map/ppermute | solution.py:302

commit v5 on v4

--- a/solution.py
+++ b/solution.py
@@ -124,87 +124,96 @@
 
 
 def attend(place_ref, col_ref, *refs):
-    *queries, out_ref, kt_ref, v_ref, s_ref, p_ref, l_ref, h_ref = refs
+    *queries, out_hbm, k_ref, v_ref, s_ref, p_ref, l_ref, h_ref, out_ref, sems = refs
     y, x, begin = place_ref[0], place_ref[1], place_ref[2]
-    for j in range(NY):
-        b = (y + j) % NY
-        kt_ref[:, j * PAGE : (j + 1) * PAGE] = col_ref[b, :PAGE, :HD].T
-        v_ref[j * PAGE : (j + 1) * PAGE] = col_ref[b, :PAGE, HD:]
-    kt_ref[:, SLAB:] = col_ref[:, PAGE:, :HD].reshape(NY * PRE, HD).T
-    v_ref[SLAB:] = col_ref[:, PAGE:, HD:].reshape(NY * PRE, HD)
-
-    c = lax.broadcasted_iota(jnp.int32, (1, KEYS), 1)
-    b = (y + c // PAGE) % NY
-    i = c - SLAB
-    slab_bias = jnp.where(c < PAGE, 0.0, jnp.where(b < y, 0.0, masked))
+    for at, j in [(0, 0)] + [(PAGE + NY * PRE + (j - 1) * PAGE, j) for j in range(1, NY)]:
+        b = (y - j + NY) % NY
+        k_ref[at : at + PAGE] = col_ref[b, :PAGE, :HD]
+        v_ref[at : at + PAGE] = col_ref[b, :PAGE, HD:]
+    shared = slice(PAGE, PAGE + NY * PRE)
+    k_ref[shared] = col_ref[:, PAGE:, :HD].reshape(NY * PRE, HD)
+    v_ref[shared] = col_ref[:, PAGE:, HD:].reshape(NY * PRE, HD)
+
+    i = lax.broadcasted_iota(jnp.int32, (1, NY * PRE), 1)
     prefix_bias = jnp.where(((i // PRE) * NX + x) * PRE + i % PRE < begin, 0.0, masked)
-    bias = jnp.where(c < SLAB, slab_bias, prefix_bias)
     token = lax.broadcasted_iota(jnp.int32, (CHUNK, PAGE), 0) % PAGE
     own_key = lax.broadcasted_iota(jnp.int32, (CHUNK, PAGE), 1)
     lane = lax.broadcasted_iota(jnp.int32, (PAGE, HD), 1)
     per_set = ROWS // CHUNK
     total = NX * per_set
 
-    def score(t):
-        n, part = divmod(t, per_set)
-        q = queries[n][part * CHUNK : (part + 1) * CHUNK]
-        s = jnp.dot(q, kt_ref[...], preferred_element_type=f32) + bias
-        at = slice(t % 2 * CHUNK, (t % 2 + 1) * CHUNK)
-        if n == 0:
-            s_ref[at, :PAGE] = jnp.where(own_key <= token, s[:, :PAGE], masked)
-        else:
-            s_ref[at, :PAGE] = s[:, :PAGE] + jnp.where((x + n) % NX > x, 0.0, masked)
-        s_ref[at, PAGE:] = s[:, PAGE:]
-
-    def weigh(t):
-        at = slice(t % 2 * CHUNK, (t % 2 + 1) * CHUNK)
-        s = s_ref[at, :]
-        top = s[:, :HD]
-        for n in range(1, KEYS // HD):
-            top = jnp.maximum(top, s[:, n * HD : (n + 1) * HD])
-        high = jnp.max(top, axis=1, keepdims=True) * to_exp2
-        p = jnp.exp2(s * to_exp2 - high)
-        mass = p[:, :HD]
-        for n in range(1, KEYS // HD):
-            mass = mass + p[:, n * HD : (n + 1) * HD]
-        l_ref[at, :] = mass
-        h_ref[at, :] = jnp.broadcast_to(high, (CHUNK, HD))
-        p_ref[at, :] = p.astype(bf16)
-
-    def gather(t, stats):
-        n, part = divmod(t, per_set)
-
-        def put(g, value):
-            out_ref[:, (x + n) % NX, g * TOK : (g + 1) * TOK] = value.reshape(KVH, TOK, HD)
-
-        at = slice(t % 2 * CHUNK, (t % 2 + 1) * CHUNK)
-        num = jnp.dot(p_ref[at, :], v_ref[...], preferred_element_type=f32)
-        mass = jnp.sum(l_ref[at, :], axis=1, keepdims=True)
-        done = (num / mass).astype(bf16)
-        level = h_ref[at, :] + jnp.log2(mass)
-        for m in range(CHUNK // PAGE):
-            g = part * (CHUNK // PAGE) + m
-            rows = slice(m * PAGE, (m + 1) * PAGE)
-            put(g, done[rows])
-            one = level[rows]
-            for piece in range(3):
-                rounded = one.astype(bf16).astype(f32)
-                stats = jnp.where(lane == piece * GROUP + g, rounded, stats)
-                one = one - rounded
-        if part == per_set - 1:
-            put(GROUP, stats.astype(bf16))
-        return stats
-
-    stats = None
-    for t in range(total + 2):
-        if t >= 2:
-            if (t - 2) % per_set == 0:
-                stats = jnp.zeros((PAGE, HD), f32)
-            stats = gather(t - 2, stats)
-        if t < total:
-            score(t)
-        if 1 <= t < total + 1:
-            weigh(t - 1)
+    def run(blocks):
+        keys = PAGE + NY * PRE + blocks * PAGE
+        last_bias = jnp.where(y >= blocks, 0.0, masked)
+
+        def score(t):
+            n, part = divmod(t, per_set)
+            q = queries[n][part * CHUNK : (part + 1) * CHUNK]
+            s = lax.dot_general(q, k_ref[:keys], (((1,), (1,)), ((), ())), preferred_element_type=f32)
+            at = slice(t % 2 * CHUNK, (t % 2 + 1) * CHUNK)
+            if n == 0:
+                s_ref[at, :PAGE] = jnp.where(own_key <= token, s[:, :PAGE], masked)
+            else:
+                s_ref[at, :PAGE] = s[:, :PAGE] + jnp.where((x + n) % NX > x, 0.0, masked)
+            s_ref[at, shared] = s[:, shared] + prefix_bias
+            if blocks > 1:
+                s_ref[at, shared.stop : keys - PAGE] = s[:, shared.stop : keys - PAGE]
+            s_ref[at, keys - PAGE : keys] = s[:, keys - PAGE :] + last_bias
+
+        def weigh(t):
+            at = slice(t % 2 * CHUNK, (t % 2 + 1) * CHUNK)
+            s = s_ref[at, :keys]
+            top = s[:, :HD]
+            for n in range(1, keys // HD):
+                top = jnp.maximum(top, s[:, n * HD : (n + 1) * HD])
+            high = jnp.max(top, axis=1, keepdims=True) * to_exp2
+            p = jnp.exp2(s * to_exp2 - high)
+            mass = p[:, :HD]
+            for n in range(1, keys // HD):
+                mass = mass + p[:, n * HD : (n + 1) * HD]
+            l_ref[at, :] = mass
+            h_ref[at, :] = jnp.broadcast_to(high, (CHUNK, HD))
+            p_ref[at, :keys] = p.astype(bf16)
+
+        def send(n):
+            return pltpu.make_async_copy(out_ref.at[n], out_hbm.at[:, (x + n) % NX], sems.at[n])
+
+        def gather(t, levels):
+            n, part = divmod(t, per_set)
+            at = slice(t % 2 * CHUNK, (t % 2 + 1) * CHUNK)
+            num = jnp.dot(p_ref[at, :keys], v_ref[:keys], preferred_element_type=f32)
+            mass = jnp.sum(l_ref[at, :], axis=1, keepdims=True)
+            done = (num / mass).astype(bf16)
+            level = h_ref[at, :] + jnp.log2(mass)
+            for m in range(CHUNK // PAGE):
+                g = part * (CHUNK // PAGE) + m
+                rows = slice(m * PAGE, (m + 1) * PAGE)
+                out_ref[n, :, g * TOK : (g + 1) * TOK] = done[rows].reshape(KVH, TOK, HD)
+                levels = jnp.where(lane == g, level[rows], levels)
+            if part == per_set - 1:
+                high = levels.astype(bf16).astype(f32)
+                rest = levels - high
+                middle = rest.astype(bf16).astype(f32)
+                stats = high + pltpu.roll(middle, GROUP, 1) + pltpu.roll(rest - middle, 2 * GROUP, 1)
+                out_ref[n, :, GROUP * TOK :] = stats.astype(bf16).reshape(KVH, TOK, HD)
+                send(n).start()
+            return levels
+
+        levels = None
+        for t in range(total + 2):
+            if t >= 2:
+                if (t - 2) % per_set == 0:
+                    levels = jnp.zeros((PAGE, HD), f32)
+                levels = gather(t - 2, levels)
+            if t < total:
+                score(t)
+            if 1 <= t < total + 1:
+                weigh(t - 1)
+        for n in range(NX):
+            send(n).wait()
+
+    for rows in range(NY // 2):
+        pl.when(y // 2 == rows)(lambda rows=rows: run(2 * rows + 1))
 
 
 def combine(in_ref, out_ref):
@@ -275,14 +284,16 @@
         attend,
         out_shape=shaped((KVH, NX, MESSAGE, HD)),
         in_specs=[spec(SMEM)] + [spec()] * (1 + NX),
-        out_specs=spec(),
+        out_specs=spec(pltpu.HBM),
         scratch_shapes=[
-            VMEM((HD, KEYS), bf16),
+            VMEM((KEYS, HD), bf16),
             VMEM((KEYS, HD), bf16),
             VMEM((2 * CHUNK, KEYS), f32),
             VMEM((2 * CHUNK, KEYS), bf16),
             VMEM((2 * CHUNK, HD), f32),
             VMEM((2 * CHUNK, HD), f32),
+            VMEM((NX, KVH, MESSAGE, HD), bf16),
+            pltpu.SemaphoreType.DMA((NX,)),
         ],
         compiler_params=params(),
         cost_estimate=cost(4 * NX * ROWS * KEYS * HD, 4 << 20, NX * ROWS * KEYS),

time: 103 us -> 101 us (0.981)
  the two profiles are of different devices: /device:TPU:6 before, /device:TPU:50 now
where the time goes in v5:
time: 101 us; the launch traced here: 100 us
  starting transfers between devices  33.5 us (33%)
  waiting for transfers between devices  25.3 us (25%)
  blocking collectives  23.6 us (23%)
  Pallas kernels  16.1 us (16%)
  between operations  1.41 us (1%)
    all_to_all x1, blocking collectives, on_device(): grouped = lax.all_to_all(packed, 'seq', 0, 0, tiled=True)  23.6 us
    ppermute x3, starting transfers between devices, on_device(): lax.ppermute(q_own, 'x', [(i, (i - k) % NX) for i in range(NX)])  10.5 us
    ppermute x3, starting transfers between devices, on_device(): lax.ppermute(offered[k], 'x', [(i, (i + k) % NX) for i in range(NX)])  10.4 us
    all_to_all x1, waiting for transfers between devices, on_device(): lax.all_to_all(parts.reshape(KVH * NX, MESSAGE, HD), ('seq', 'x'), 0, 0,...  9.16 us
    pallas_call x1, Pallas kernels, on_device(): pl.pallas_call(attend, out_shape=shaped((KVH, NX, MESSAGE, HD)), in_specs...  9.1 us
    ppermute x3, waiting for transfers between devices, on_device(): lax.ppermute(offered[k], 'x', [(i, (i + k) % NX) for i in range(NX)])  9 us
    ppermute x3, waiting for transfers between devices, on_device(): lax.ppermute(q_own, 'x', [(i, (i - k) % NX) for i in range(NX)])  7.15 us
    all_to_all x1, starting transfers between devices, on_device(): column = lax.all_to_all(kv_send, 'y', 0, 0, tiled=True)  6.98 us
  transfers between devices with their start and end apart: 8, of which 6 were waited for; matrix products, arithmetic and copies ran while one was open for 0% of the time, Pallas kernels for 2%

profile of v5, /device:TPU:50, one launch (start us, length us, event | category | flops | bytes accessed | tf_op | source)
XLA Modules:
  0.0 100.0 jit_solution(15245736728285121404)
XLA Ops:
  0.6 0.0 copy-start
  1.3 1.9 %pack.1 = bf16[8,16,1280]{2,1,0:T(8,128)(2,1)} custom-call(s32[1]{0:T(128)S(6)} %copy.8.offset_ref, bf16[16,8192]{1,0:T(8,128)(2,1)} %bitcast.8, bf16[16,2048]{1,0:T(8,128)(2,1)} %bitcast.10), custom_call_target="tpu_custom_call" | custom-call | tf_op jit(solution)/shard_map/pack/pallas_call | solution.py:261
  3.2 23.6 %all_to_all.15.in_ref = bf16[8,16,1280]{2,1,0:T(8,128)(2,1)S(1)} all-to-all(bf16[8,16,1280]{2,1,0:T(8,128)(2,1)} %pack.1), channel_id=1, replica_groups=mesh['seq'=8,'y'=8,'x'=4,'rep'=2] {'seq'}, dimensions={0} | all-to-all | bytes 655360 | tf_op jit(solution)/shard_map/all_to_all | solution.py:270
  26.8 0.0 copy-done
  26.8 0.9 spread.1
  27.7 7.0 %all-to-all-start.1 = ((bf16[8,160,256]{2,1,0:T(8,128)(2,1)}), bf16[8,160,256]{2,1,0:T(8,128)(2,1)S(1)}, u32[]{:S(2)}, u32[]{:S(2)}) async-start(bf16[8,160,256]{2,1,0:T(8,128)(2,1)} %get-tuple-element.11), calls=%async_computation.1 | async-start | bytes 1310720 | tf_op jit(solution)/shard_map/all_to_all | solution.py:280
  34.7 3.4 %collective-permute-start.2 = (bf16[1024,128]{1,0:T(8,128)(2,1)S(1)}, bf16[1024,128]{1,0:T(8,128)(2,1)S(1)}, u32[]{:S(2)}, u32[]{:S(2)}) collective-permute-start(bf16[1024,128]{1,0:T(8,128)(2,1)S(1)} %get-tuple-element.12.refs_0_), channel_id=1, source_target_pairs={{0,2},{2,4},{4,6},{6,0},{1,3},{3,5},{5,7},{7,1},{8,10},{10,12},{12... | collective-permute-start | bytes 786440 | tf_op jit(solution)/shard_map/ppermute | solution.py:281
  38.1 3.0 %collective-permute-start.1 = (bf16[1024,128]{1,0:T(8,128)(2,1)S(1)}, bf16[1024,128]{1,0:T(8,128)(2,1)S(1)}, u32[]{:S(2)}, u32[]{:S(2)}) collective-permute-start(bf16[1024,128]{1,0:T(8,128)(2,1)S(1)} %get-tuple-element.12.refs_0_), channel_id=1, source_target_pairs={{0,4},{2,6},{4,0},{6,2},{1,5},{3,7},{5,1},{7,3},{8,12},{10,14},{12... | collective-permute-start | bytes 786440 | tf_op jit(solution)/shard_map/ppermute | solution.py:281
  41.1 4.1 %collective-permute-start = (bf16[1024,128]{1,0:T(8,128)(2,1)S(1)}, bf16[1024,128]{1,0:T(8,128)(2,1)S(1)}, u32[]{:S(2)}, u32[]{:S(2)}) collective-permute-start(bf16[1024,128]{1,0:T(8,128)(2,1)S(1)} %get-tuple-element.12.refs_0_), channel_id=1, source_target_pairs={{0,6},{2,0},{4,2},{6,4},{1,7},{3,1},{5,3},{7,5},{8,14},{10,8},{12,... | collective-permute-start | bytes 786440 | tf_op jit(solution)/shard_map/ppermute | solution.py:281
  45.2 0.1 pad_add_fusion.place_ref
  45.3 0.0 collective-permute-done.2.refs_3_
  45.3 4.5 %collective-permute-done.1.refs_2_ = bf16[1024,128]{1,0:T(8,128)(2,1)S(1)} collective-permute-done((bf16[1024,128]{1,0:T(8,128)(2,1)S(1)}, bf16[1024,128]{1,0:T(8,128)(2,1)S(1)}, u32[]{:S(2)}, u32[]{:S(2)}) %collective-permute-start.1) | collective-permute-done | bytes 262176 | tf_op jit(solution)/shard_map/ppermute | solution.py:281
  49.7 2.7 %collective-permute-done.refs_1_ = bf16[1024,128]{1,0:T(8,128)(2,1)S(1)} collective-permute-done((bf16[1024,128]{1,0:T(8,128)(2,1)S(1)}, bf16[1024,128]{1,0:T(8,128)(2,1)S(1)}, u32[]{:S(2)}, u32[]{:S(2)}) %collective-permute-start) | collective-permute-done | bytes 262176 | tf_op jit(solution)/shard_map/ppermute | solution.py:281
  52.4 0.0 all-to-all-done.1.col_ref
  52.4 9.1 %attend.1 = bf16[8,4,144,128]{3,2,1,0:T(8,128)(2,1)} custom-call(s32[3]{0:T(128)S(1)} %pad_add_fusion.place_ref, bf16[8,160,256]{2,1,0:T(8,128)(2,1)S(1)} %all-to-all-done.1.col_ref, bf16[1024,128]{1,0:T(8,128)(2,1)S(1)} %get-tuple-element.12.refs_0_, bf16[1024,128]{1,0:T(8,128)(2,1)S(1)} %collective-permute-done.refs_1_, ...), custom_call_target="tpu_custom_call" | custom-call | flops 2684354560 | bytes 4194304 | tf_op jit(solution)/shard_map/attend/pallas_call | solution.py:283
  61.5 0.0 copy-start.1
  61.6 5.6 %all-to-all-start.2 = ((bf16[32,144,128]{2,1,0:T(8,128)(2,1)}), bf16[32,144,128]{2,1,0:T(8,128)(2,1)S(1)}, u32[]{:S(2)}, u32[]{:S(2)}) async-start(bf16[32,144,128]{2,1,0:T(8,128)(2,1)} %bitcast.4), calls=%async_computation.2 | async-start | bytes 2359296 | tf_op jit(solution)/shard_map/all_to_all | solution.py:302
  67.2 0.0 copy-done.1
  67.2 0.9 offer_pages.1
  68.1 3.4 %collective-permute-start.3 = (bf16[272,256]{1,0:T(8,128)(2,1)S(1)}, bf16[272,256]{1,0:T(8,128)(2,1)S(1)}, u32[]{:S(2)}, u32[]{:S(2)}) collective-permute-start(bf16[272,256]{1,0:T(8,128)(2,1)S(1)} %get-tuple-element.14), channel_id=1, source_target_pairs={{0,2},{2,4},{4,6},{6,0},{1,3},{3,5},{5,7},{7,1},{8,10},{10,12},{12... | collective-permute-start | bytes 417800 | tf_op jit(solution)/shard_map/ppermute | solution.py:313
  71.5 2.7 %collective-permute-start.4 = (bf16[272,256]{1,0:T(8,128)(2,1)S(1)}, bf16[272,256]{1,0:T(8,128)(2,1)S(1)}, u32[]{:S(2)}, u32[]{:S(2)}) collective-permute-start(bf16[272,256]{1,0:T(8,128)(2,1)S(1)} %get-tuple-element.15), channel_id=1, source_target_pairs={{0,4},{2,6},{4,0},{6,2},{1,5},{3,7},{5,1},{7,3},{8,12},{10,14},{12... | collective-permute-start | bytes 417800 | tf_op jit(solution)/shard_map/ppermute | solution.py:313
  74.2 4.3 %collective-permute-start.5 = (bf16[272,256]{1,0:T(8,128)(2,1)S(1)}, bf16[272,256]{1,0:T(8,128)(2,1)S(1)}, u32[]{:S(2)}, u32[]{:S(2)}) collective-permute-start(bf16[272,256]{1,0:T(8,128)(2,1)S(1)} %get-tuple-element.16), channel_id=1, source_target_pairs={{0,6},{2,0},{4,2},{6,4},{1,7},{3,1},{5,3},{7,5},{8,14},{10,8},{12,... | collective-permute-start | bytes 417800 | tf_op jit(solution)/shard_map/ppermute | solution.py:313
  78.5 0.3 collective-permute-done.3.refs_1_
  78.8 4.8 %collective-permute-done.4.refs_2_ = bf16[272,256]{1,0:T(8,128)(2,1)S(1)} collective-permute-done((bf16[272,256]{1,0:T(8,128)(2,1)S(1)}, bf16[272,256]{1,0:T(8,128)(2,1)S(1)}, u32[]{:S(2)}, u32[]{:S(2)}) %collective-permute-start.4) | collective-permute-done | bytes 139296 | tf_op jit(solution)/shard_map/ppermute | solution.py:313
  83.6 3.9 %collective-permute-done.5.refs_3_ = bf16[272,256]{1,0:T(8,128)(2,1)S(1)} collective-permute-done((bf16[272,256]{1,0:T(8,128)(2,1)S(1)}, bf16[272,256]{1,0:T(8,128)(2,1)S(1)}, u32[]{:S(2)}, u32[]{:S(2)}) %collective-permute-start.5) | collective-permute-done | bytes 139296 | tf_op jit(solution)/shard_map/ppermute | solution.py:313
  87.5 0.8 keep_pages.1
  88.3 9.2 %all-to-all-done.2.in_ref = bf16[32,144,128]{2,1,0:T(8,128)(2,1)S(1)} async-done(((bf16[32,144,128]{2,1,0:T(8,128)(2,1)}), bf16[32,144,128]{2,1,0:T(8,128)(2,1)S(1)}, u32[]{:S(2)}, u32[]{:S(2)}) %all-to-all-start.2) | async-done | bytes 1179680 | tf_op jit(solution)/shard_map/all_to_all | solution.py:302
  97.5 2.5 %combine.1 = bf16[16,8192]{1,0:T(8,128)(2,1)} custom-call(bf16[32,144,128]{2,1,0:T(8,128)(2,1)S(1)} %all-to-all-done.2.in_ref), custom_call_target="tpu_custom_call" | custom-call | tf_op jit(solution)/shard_map/combine/pallas_call | solution.py:323
Async XLA Ops:
  0.6 26.2 %copy-start = (bf16[32,256]{1,0:T(8,128)(2,1)S(1)}, bf16[32,256]{1,0:T(8,128)(2,1)}, u32[]{:S(2)}) copy-start(bf16[32,256]{1,0:T(8,128)(2,1)} %pre_ref.1) | copy-start | bytes 49156
  27.7 24.7 %all-to-all-start.1 = ((bf16[8,160,256]{2,1,0:T(8,128)(2,1)}), bf16[8,160,256]{2,1,0:T(8,128)(2,1)S(1)}, u32[]{:S(2)}, u32[]{:S(2)}) async-start(bf16[8,160,256]{2,1,0:T(8,128)(2,1)} %get-tuple-element.11), calls=%async_computation.1 | async-start | bytes 1310720 | tf_op jit(solution)/shard_map/all_to_all | solution.py:280
  34.7 10.6 %collective-permute-start.2 = (bf16[1024,128]{1,0:T(8,128)(2,1)S(1)}, bf16[1024,128]{1,0:T(8,128)(2,1)S(1)}, u32[]{:S(2)}, u32[]{:S(2)}) collective-permute-start(bf16[1024,128]{1,0:T(8,128)(2,1)S(1)} %get-tuple-element.12.refs_0_), channel_id=1, source_target_pairs={{0,2},{2,4},{4,6},{6,0},{1,3},{3,5},{5,7},{7,1},{8,10},{10,12},{12... | collective-permute-start | bytes 786440 | tf_op jit(solution)/shard_map/ppermute | solution.py:281
  38.1 11.6 %collective-permute-start.1 = (bf16[1024,128]{1,0:T(8,128)(2,1)S(1)}, bf16[1024,128]{1,0:T(8,128)(2,1)S(1)}, u32[]{:S(2)}, u32[]{:S(2)}) collective-permute-start(bf16[1024,128]{1,0:T(8,128)(2,1)S(1)} %get-tuple-element.12.refs_0_), channel_id=1, source_target_pairs={{0,4},{2,6},{4,0},{6,2},{1,5},{3,7},{5,1},{7,3},{8,12},{10,14},{12... | collective-permute-start | bytes 786440 | tf_op jit(solution)/shard_map/ppermute | solution.py:281
  41.1 11.3 %collective-permute-start = (bf16[1024,128]{1,0:T(8,128)(2,1)S(1)}, bf16[1024,128]{1,0:T(8,128)(2,1)S(1)}, u32[]{:S(2)}, u32[]{:S(2)}) collective-permute-start(bf16[1024,128]{1,0:T(8,128)(2,1)S(1)} %get-tuple-element.12.refs_0_), channel_id=1, source_target_pairs={{0,6},{2,0},{4,2},{6,4},{1,7},{3,1},{5,3},{7,5},{8,14},{10,8},{12,... | collective-permute-start | bytes 786440 | tf_op jit(solution)/shard_map/ppermute | solution.py:281
  61.5 5.6 %copy-start.1 = (s32[1,32]{1,0:T(1,128)S(1)}, s32[1,32]{1,0:T(1,128)}, u32[]{:S(2)}) copy-start(s32[1,32]{1,0:T(1,128)} %own_ref.1) | copy-start | bytes 388
  61.6 35.9 %all-to-all-start.2 = ((bf16[32,144,128]{2,1,0:T(8,128)(2,1)}), bf16[32,144,128]{2,1,0:T(8,128)(2,1)S(1)}, u32[]{:S(2)}, u32[]{:S(2)}) async-start(bf16[32,144,128]{2,1,0:T(8,128)(2,1)} %bitcast.4), calls=%async_computation.2 | async-start | bytes 2359296 | tf_op jit(solution)/shard_map/all_to_all | solution.py:302
  68.1 10.7 %collective-permute-start.3 = (bf16[272,256]{1,0:T(8,128)(2,1)S(1)}, bf16[272,256]{1,0:T(8,128)(2,1)S(1)}, u32[]{:S(2)}, u32[]{:S(2)}) collective-permute-start(bf16[272,256]{1,0:T(8,128)(2,1)S(1)} %get-tuple-element.14), channel_id=1, source_target_pairs={{0,2},{2,4},{4,6},{6,0},{1,3},{3,5},{5,7},{7,1},{8,10},{10,12},{12... | collective-permute-start | bytes 417800 | tf_op jit(solution)/shard_map/ppermute | solution.py:313
  71.5 12.2 %collective-permute-start.4 = (bf16[272,256]{1,0:T(8,128)(2,1)S(1)}, bf16[272,256]{1,0:T(8,128)(2,1)S(1)}, u32[]{:S(2)}, u32[]{:S(2)}) collective-permute-start(bf16[272,256]{1,0:T(8,128)(2,1)S(1)} %get-tuple-element.15), channel_id=1, source_target_pairs={{0,4},{2,6},{4,0},{6,2},{1,5},{3,7},{5,1},{7,3},{8,12},{10,14},{12... | collective-permute-start | bytes 417800 | tf_op jit(solution)/shard_map/ppermute | solution.py:313
  74.2 13.3 %collective-permute-start.5 = (bf16[272,256]{1,0:T(8,128)(2,1)S(1)}, bf16[272,256]{1,0:T(8,128)(2,1)S(1)}, u32[]{:S(2)}, u32[]{:S(2)}) collective-permute-start(bf16[272,256]{1,0:T(8,128)(2,1)S(1)} %get-tuple-element.16), channel_id=1, source_target_pairs={{0,6},{2,0},{4,2},{6,4},{1,7},{3,1},{5,3},{7,5},{8,14},{10,8},{12,... | collective-permute-start | bytes 417800 | tf_op jit(solution)/shard_map/ppermute | solution.py:313

commit v6 on v5

--- a/solution.py
+++ b/solution.py
@@ -134,7 +134,9 @@
     k_ref[shared] = col_ref[:, PAGE:, :HD].reshape(NY * PRE, HD)
     v_ref[shared] = col_ref[:, PAGE:, HD:].reshape(NY * PRE, HD)
 
-    i = lax.broadcasted_iota(jnp.int32, (1, NY * PRE), 1)
+    always = slice(PAGE, 2 * PAGE)
+    perhaps = slice(2 * PAGE, PAGE + NY * PRE)
+    i = lax.broadcasted_iota(jnp.int32, (1, NY * PRE - PAGE), 1) + PAGE
     prefix_bias = jnp.where(((i // PRE) * NX + x) * PRE + i % PRE < begin, 0.0, masked)
     token = lax.broadcasted_iota(jnp.int32, (CHUNK, PAGE), 0) % PAGE
     own_key = lax.broadcasted_iota(jnp.int32, (CHUNK, PAGE), 1)
@@ -155,7 +157,8 @@
                 s_ref[at, :PAGE] = jnp.where(own_key <= token, s[:, :PAGE], masked)
             else:
                 s_ref[at, :PAGE] = s[:, :PAGE] + jnp.where((x + n) % NX > x, 0.0, masked)
-            s_ref[at, shared] = s[:, shared] + prefix_bias
+            s_ref[at, always] = s[:, always]
+            s_ref[at, perhaps] = s[:, perhaps] + prefix_bias
             if blocks > 1:
                 s_ref[at, shared.stop : keys - PAGE] = s[:, shared.stop : keys - PAGE]
             s_ref[at, keys - PAGE : keys] = s[:, keys - PAGE :] + last_bias

time: 101 us -> 101 us (level)
  no operation moved by 1% of the time
where the time goes in v6:
time: 101 us; the launch traced here: 100 us
  starting transfers between devices  33.5 us (33%)
  waiting for transfers between devices  25.3 us (25%)
  blocking collectives  23.6 us (23%)
  Pallas kernels  16.1 us (16%)
  between operations  1.41 us (1%)
    all_to_all x1, blocking collectives, on_device(): grouped = lax.all_to_all(packed, 'seq', 0, 0, tiled=True)  23.6 us
    ppermute x3, starting transfers between devices, on_device(): lax.ppermute(q_own, 'x', [(i, (i - k) % NX) for i in range(NX)])  10.5 us
    ppermute x3, starting transfers between devices, on_device(): lax.ppermute(offered[k], 'x', [(i, (i + k) % NX) for i in range(NX)])  10.4 us
    all_to_all x1, waiting for transfers between devices, on_device(): lax.all_to_all(parts.reshape(KVH * NX, MESSAGE, HD), ('seq', 'x'), 0, 0,...  9.16 us
    pallas_call x1, Pallas kernels, on_device(): pl.pallas_call(attend, out_shape=shaped((KVH, NX, MESSAGE, HD)), in_specs...  9.13 us
    ppermute x3, waiting for transfers between devices, on_device(): lax.ppermute(offered[k], 'x', [(i, (i + k) % NX) for i in range(NX)])  9 us
    ppermute x3, waiting for transfers between devices, on_device(): lax.ppermute(q_own, 'x', [(i, (i - k) % NX) for i in range(NX)])  7.15 us
    all_to_all x1, starting transfers between devices, on_device(): column = lax.all_to_all(kv_send, 'y', 0, 0, tiled=True)  6.98 us
  transfers between devices with their start and end apart: 8, of which 6 were waited for; matrix products, arithmetic and copies ran while one was open for 0% of the time, Pallas kernels for 2%

profile of v6, /device:TPU:50, one launch (start us, length us, event | category | flops | bytes accessed | tf_op | source)
XLA Modules:
  0.0 100.0 jit_solution(147578162377493665)
XLA Ops:
  0.6 0.0 copy-start
  1.3 1.9 %pack.1 = bf16[8,16,1280]{2,1,0:T(8,128)(2,1)} custom-call(s32[1]{0:T(128)S(6)} %copy.8.offset_ref, bf16[16,8192]{1,0:T(8,128)(2,1)} %bitcast.8, bf16[16,2048]{1,0:T(8,128)(2,1)} %bitcast.10), custom_call_target="tpu_custom_call" | custom-call | tf_op jit(solution)/shard_map/pack/pallas_call | solution.py:264
  3.2 23.6 %all_to_all.15.in_ref = bf16[8,16,1280]{2,1,0:T(8,128)(2,1)S(1)} all-to-all(bf16[8,16,1280]{2,1,0:T(8,128)(2,1)} %pack.1), channel_id=1, replica_groups=mesh['seq'=8,'y'=8,'x'=4,'rep'=2] {'seq'}, dimensions={0} | all-to-all | bytes 655360 | tf_op jit(solution)/shard_map/all_to_all | solution.py:273
  26.8 0.0 copy-done
  26.8 0.9 spread.1
  27.7 7.0 %all-to-all-start.1 = ((bf16[8,160,256]{2,1,0:T(8,128)(2,1)}), bf16[8,160,256]{2,1,0:T(8,128)(2,1)S(1)}, u32[]{:S(2)}, u32[]{:S(2)}) async-start(bf16[8,160,256]{2,1,0:T(8,128)(2,1)} %get-tuple-element.11), calls=%async_computation.1 | async-start | bytes 1310720 | tf_op jit(solution)/shard_map/all_to_all | solution.py:283
  34.7 3.4 %collective-permute-start.2 = (bf16[1024,128]{1,0:T(8,128)(2,1)S(1)}, bf16[1024,128]{1,0:T(8,128)(2,1)S(1)}, u32[]{:S(2)}, u32[]{:S(2)}) collective-permute-start(bf16[1024,128]{1,0:T(8,128)(2,1)S(1)} %get-tuple-element.12.refs_0_), channel_id=1, source_target_pairs={{0,2},{2,4},{4,6},{6,0},{1,3},{3,5},{5,7},{7,1},{8,10},{10,12},{12... | collective-permute-start | bytes 786440 | tf_op jit(solution)/shard_map/ppermute | solution.py:284
  38.1 3.0 %collective-permute-start.1 = (bf16[1024,128]{1,0:T(8,128)(2,1)S(1)}, bf16[1024,128]{1,0:T(8,128)(2,1)S(1)}, u32[]{:S(2)}, u32[]{:S(2)}) collective-permute-start(bf16[1024,128]{1,0:T(8,128)(2,1)S(1)} %get-tuple-element.12.refs_0_), channel_id=1, source_target_pairs={{0,4},{2,6},{4,0},{6,2},{1,5},{3,7},{5,1},{7,3},{8,12},{10,14},{12... | collective-permute-start | bytes 786440 | tf_op jit(solution)/shard_map/ppermute | solution.py:284
  41.1 4.1 %collective-permute-start = (bf16[1024,128]{1,0:T(8,128)(2,1)S(1)}, bf16[1024,128]{1,0:T(8,128)(2,1)S(1)}, u32[]{:S(2)}, u32[]{:S(2)}) collective-permute-start(bf16[1024,128]{1,0:T(8,128)(2,1)S(1)} %get-tuple-element.12.refs_0_), channel_id=1, source_target_pairs={{0,6},{2,0},{4,2},{6,4},{1,7},{3,1},{5,3},{7,5},{8,14},{10,8},{12,... | collective-permute-start | bytes 786440 | tf_op jit(solution)/shard_map/ppermute | solution.py:284
  45.2 0.1 pad_add_fusion.place_ref
  45.3 0.0 collective-permute-done.2.refs_3_
  45.3 4.5 %collective-permute-done.1.refs_2_ = bf16[1024,128]{1,0:T(8,128)(2,1)S(1)} collective-permute-done((bf16[1024,128]{1,0:T(8,128)(2,1)S(1)}, bf16[1024,128]{1,0:T(8,128)(2,1)S(1)}, u32[]{:S(2)}, u32[]{:S(2)}) %collective-permute-start.1) | collective-permute-done | bytes 262176 | tf_op jit(solution)/shard_map/ppermute | solution.py:284
  49.7 2.7 %collective-permute-done.refs_1_ = bf16[1024,128]{1,0:T(8,128)(2,1)S(1)} collective-permute-done((bf16[1024,128]{1,0:T(8,128)(2,1)S(1)}, bf16[1024,128]{1,0:T(8,128)(2,1)S(1)}, u32[]{:S(2)}, u32[]{:S(2)}) %collective-permute-start) | collective-permute-done | bytes 262176 | tf_op jit(solution)/shard_map/ppermute | solution.py:284
  52.4 0.0 all-to-all-done.1.col_ref
  52.4 9.1 %attend.1 = bf16[8,4,144,128]{3,2,1,0:T(8,128)(2,1)} custom-call(s32[3]{0:T(128)S(1)} %pad_add_fusion.place_ref, bf16[8,160,256]{2,1,0:T(8,128)(2,1)S(1)} %all-to-all-done.1.col_ref, bf16[1024,128]{1,0:T(8,128)(2,1)S(1)} %get-tuple-element.12.refs_0_, bf16[1024,128]{1,0:T(8,128)(2,1)S(1)} %collective-permute-done.refs_1_, ...), custom_call_target="tpu_custom_call" | custom-call | flops 2684354560 | bytes 4194304 | tf_op jit(solution)/shard_map/attend/pallas_call | solution.py:286
  61.6 0.0 copy-start.1
  61.6 5.6 %all-to-all-start.2 = ((bf16[32,144,128]{2,1,0:T(8,128)(2,1)}), bf16[32,144,128]{2,1,0:T(8,128)(2,1)S(1)}, u32[]{:S(2)}, u32[]{:S(2)}) async-start(bf16[32,144,128]{2,1,0:T(8,128)(2,1)} %bitcast.4), calls=%async_computation.2 | async-start | bytes 2359296 | tf_op jit(solution)/shard_map/all_to_all | solution.py:305
  67.2 0.0 copy-done.1
  67.2 0.9 offer_pages.1
  68.1 3.4 %collective-permute-start.3 = (bf16[272,256]{1,0:T(8,128)(2,1)S(1)}, bf16[272,256]{1,0:T(8,128)(2,1)S(1)}, u32[]{:S(2)}, u32[]{:S(2)}) collective-permute-start(bf16[272,256]{1,0:T(8,128)(2,1)S(1)} %get-tuple-element.14), channel_id=1, source_target_pairs={{0,2},{2,4},{4,6},{6,0},{1,3},{3,5},{5,7},{7,1},{8,10},{10,12},{12... | collective-permute-start | bytes 417800 | tf_op jit(solution)/shard_map/ppermute | solution.py:316
  71.5 2.7 %collective-permute-start.4 = (bf16[272,256]{1,0:T(8,128)(2,1)S(1)}, bf16[272,256]{1,0:T(8,128)(2,1)S(1)}, u32[]{:S(2)}, u32[]{:S(2)}) collective-permute-start(bf16[272,256]{1,0:T(8,128)(2,1)S(1)} %get-tuple-element.15), channel_id=1, source_target_pairs={{0,4},{2,6},{4,0},{6,2},{1,5},{3,7},{5,1},{7,3},{8,12},{10,14},{12... | collective-permute-start | bytes 417800 | tf_op jit(solution)/shard_map/ppermute | solution.py:316
  74.3 4.3 %collective-permute-start.5 = (bf16[272,256]{1,0:T(8,128)(2,1)S(1)}, bf16[272,256]{1,0:T(8,128)(2,1)S(1)}, u32[]{:S(2)}, u32[]{:S(2)}) collective-permute-start(bf16[272,256]{1,0:T(8,128)(2,1)S(1)} %get-tuple-element.16), channel_id=1, source_target_pairs={{0,6},{2,0},{4,2},{6,4},{1,7},{3,1},{5,3},{7,5},{8,14},{10,8},{12,... | collective-permute-start | bytes 417800 | tf_op jit(solution)/shard_map/ppermute | solution.py:316
  78.6 0.3 collective-permute-done.3.refs_1_
  78.9 4.8 %collective-permute-done.4.refs_2_ = bf16[272,256]{1,0:T(8,128)(2,1)S(1)} collective-permute-done((bf16[272,256]{1,0:T(8,128)(2,1)S(1)}, bf16[272,256]{1,0:T(8,128)(2,1)S(1)}, u32[]{:S(2)}, u32[]{:S(2)}) %collective-permute-start.4) | collective-permute-done | bytes 139296 | tf_op jit(solution)/shard_map/ppermute | solution.py:316
  83.7 3.9 %collective-permute-done.5.refs_3_ = bf16[272,256]{1,0:T(8,128)(2,1)S(1)} collective-permute-done((bf16[272,256]{1,0:T(8,128)(2,1)S(1)}, bf16[272,256]{1,0:T(8,128)(2,1)S(1)}, u32[]{:S(2)}, u32[]{:S(2)}) %collective-permute-start.5) | collective-permute-done | bytes 139296 | tf_op jit(solution)/shard_map/ppermute | solution.py:316
  87.6 0.8 keep_pages.1
  88.3 9.2 %all-to-all-done.2.in_ref = bf16[32,144,128]{2,1,0:T(8,128)(2,1)S(1)} async-done(((bf16[32,144,128]{2,1,0:T(8,128)(2,1)}), bf16[32,144,128]{2,1,0:T(8,128)(2,1)S(1)}, u32[]{:S(2)}, u32[]{:S(2)}) %all-to-all-start.2) | async-done | bytes 1179680 | tf_op jit(solution)/shard_map/all_to_all | solution.py:305
  97.5 2.5 %combine.1 = bf16[16,8192]{1,0:T(8,128)(2,1)} custom-call(bf16[32,144,128]{2,1,0:T(8,128)(2,1)S(1)} %all-to-all-done.2.in_ref), custom_call_target="tpu_custom_call" | custom-call | tf_op jit(solution)/shard_map/combine/pallas_call | solution.py:326
Async XLA Ops:
  0.6 26.2 %copy-start = (bf16[32,256]{1,0:T(8,128)(2,1)S(1)}, bf16[32,256]{1,0:T(8,128)(2,1)}, u32[]{:S(2)}) copy-start(bf16[32,256]{1,0:T(8,128)(2,1)} %pre_ref.1) | copy-start | bytes 49156
  27.7 24.7 %all-to-all-start.1 = ((bf16[8,160,256]{2,1,0:T(8,128)(2,1)}), bf16[8,160,256]{2,1,0:T(8,128)(2,1)S(1)}, u32[]{:S(2)}, u32[]{:S(2)}) async-start(bf16[8,160,256]{2,1,0:T(8,128)(2,1)} %get-tuple-element.11), calls=%async_computation.1 | async-start | bytes 1310720 | tf_op jit(solution)/shard_map/all_to_all | solution.py:283
  34.7 10.6 %collective-permute-start.2 = (bf16[1024,128]{1,0:T(8,128)(2,1)S(1)}, bf16[1024,128]{1,0:T(8,128)(2,1)S(1)}, u32[]{:S(2)}, u32[]{:S(2)}) collective-permute-start(bf16[1024,128]{1,0:T(8,128)(2,1)S(1)} %get-tuple-element.12.refs_0_), channel_id=1, source_target_pairs={{0,2},{2,4},{4,6},{6,0},{1,3},{3,5},{5,7},{7,1},{8,10},{10,12},{12... | collective-permute-start | bytes 786440 | tf_op jit(solution)/shard_map/ppermute | solution.py:284
  38.1 11.6 %collective-permute-start.1 = (bf16[1024,128]{1,0:T(8,128)(2,1)S(1)}, bf16[1024,128]{1,0:T(8,128)(2,1)S(1)}, u32[]{:S(2)}, u32[]{:S(2)}) collective-permute-start(bf16[1024,128]{1,0:T(8,128)(2,1)S(1)} %get-tuple-element.12.refs_0_), channel_id=1, source_target_pairs={{0,4},{2,6},{4,0},{6,2},{1,5},{3,7},{5,1},{7,3},{8,12},{10,14},{12... | collective-permute-start | bytes 786440 | tf_op jit(solution)/shard_map/ppermute | solution.py:284
  41.1 11.3 %collective-permute-start = (bf16[1024,128]{1,0:T(8,128)(2,1)S(1)}, bf16[1024,128]{1,0:T(8,128)(2,1)S(1)}, u32[]{:S(2)}, u32[]{:S(2)}) collective-permute-start(bf16[1024,128]{1,0:T(8,128)(2,1)S(1)} %get-tuple-element.12.refs_0_), channel_id=1, source_target_pairs={{0,6},{2,0},{4,2},{6,4},{1,7},{3,1},{5,3},{7,5},{8,14},{10,8},{12,... | collective-permute-start | bytes 786440 | tf_op jit(solution)/shard_map/ppermute | solution.py:284
  61.6 5.6 %copy-start.1 = (s32[1,32]{1,0:T(1,128)S(1)}, s32[1,32]{1,0:T(1,128)}, u32[]{:S(2)}) copy-start(s32[1,32]{1,0:T(1,128)} %own_ref.1) | copy-start | bytes 388
  61.6 35.9 %all-to-all-start.2 = ((bf16[32,144,128]{2,1,0:T(8,128)(2,1)}), bf16[32,144,128]{2,1,0:T(8,128)(2,1)S(1)}, u32[]{:S(2)}, u32[]{:S(2)}) async-start(bf16[32,144,128]{2,1,0:T(8,128)(2,1)} %bitcast.4), calls=%async_computation.2 | async-start | bytes 2359296 | tf_op jit(solution)/shard_map/all_to_all | solution.py:305
  68.1 10.7 %collective-permute-start.3 = (bf16[272,256]{1,0:T(8,128)(2,1)S(1)}, bf16[272,256]{1,0:T(8,128)(2,1)S(1)}, u32[]{:S(2)}, u32[]{:S(2)}) collective-permute-start(bf16[272,256]{1,0:T(8,128)(2,1)S(1)} %get-tuple-element.14), channel_id=1, source_target_pairs={{0,2},{2,4},{4,6},{6,0},{1,3},{3,5},{5,7},{7,1},{8,10},{10,12},{12... | collective-permute-start | bytes 417800 | tf_op jit(solution)/shard_map/ppermute | solution.py:316
  71.5 12.2 %collective-permute-start.4 = (bf16[272,256]{1,0:T(8,128)(2,1)S(1)}, bf16[272,256]{1,0:T(8,128)(2,1)S(1)}, u32[]{:S(2)}, u32[]{:S(2)}) collective-permute-start(bf16[272,256]{1,0:T(8,128)(2,1)S(1)} %get-tuple-element.15), channel_id=1, source_target_pairs={{0,4},{2,6},{4,0},{6,2},{1,5},{3,7},{5,1},{7,3},{8,12},{10,14},{12... | collective-permute-start | bytes 417800 | tf_op jit(solution)/shard_map/ppermute | solution.py:316
  74.3 13.3 %collective-permute-start.5 = (bf16[272,256]{1,0:T(8,128)(2,1)S(1)}, bf16[272,256]{1,0:T(8,128)(2,1)S(1)}, u32[]{:S(2)}, u32[]{:S(2)}) collective-permute-start(bf16[272,256]{1,0:T(8,128)(2,1)S(1)} %get-tuple-element.16), channel_id=1, source_target_pairs={{0,6},{2,0},{4,2},{6,4},{1,7},{3,1},{5,3},{7,5},{8,14},{10,8},{12,... | collective-permute-start | bytes 417800 | tf_op jit(solution)/shard_map/ppermute | solution.py:316
